TPU v7x, 32 devices: a whole 2x2x4 slice. The times are simulated.
32 devices in a mesh: gx: 8 (over y, x, core), gy: 4 (over z).
Axes of the slice: x: 2, y: 2, z: 4, core: 2. Of those that a mesh axis runs over, the one named last changes fastest.
Arguments:
- stress: float32 [6, 16, 512, 512], P(None, None, 'gx', 'gy'), may hold values from -6 to 6
- velocity: float32 [3, 16, 512, 512], P(None, None, 'gx', 'gy'), may hold values from -6 to 6
- material: int32 [16, 512, 512], P(None, 'gx', 'gy'), may hold values from 0 to 2
- layer_kind: int32 [16], replicated, may hold values from 0 to 2
- buoyancy: float32 [3], replicated, may hold values from 0.05 to 0.3
- lame_first: float32 [3], replicated, may hold values from 0.05 to 0.3
- shear_modulus: float32 [3], replicated, may hold values from 0.05 to 0.2
- piezo: float32 [3], replicated, may hold values from 0.5 to 2
- permit_lateral: float32 [3], replicated, may hold values from 0.5 to 4
- permit_normal: float32 [3], replicated, may hold values from 0.5 to 4
Outputs:
- stress_next: float32 [6, 16, 512, 512], P(None, None, 'gx', 'gy')
- velocity_next: float32 [3, 16, 512, 512], P(None, None, 'gx', 'gy')
- potential_modes: float32 [2, 16, 512, 512], P(None, None, ('gx', 'gy'))
Inputs may be any that keep to these rules, and one draw needn't show every extreme that they name: `layer_kind`: material codes of the layers, as for cells.
All inputs are finite; a program needn't handle non-finite values.
Results may differ from a plain program's by a relative error of at most 0.000076.
Values sent between devices are 32-bit elements; how exact they have to be, the bound alone decides.
A program may use at most 192 MiB of HBM per device.

v0:
```python
import math

import jax
import jax.numpy as jnp
from jax import lax
from jax.sharding import PartitionSpec as P


def extended(block, sides, width):
    for axis, dim in sides:
        count = lax.axis_size(axis)
        forward = [(i, i + 1) for i in range(count - 1)]
        backward = [(target, source) for source, target in forward]
        low = lax.ppermute(
            lax.slice_in_dim(block, block.shape[dim] - width, None, axis=dim), axis, forward
        )
        high = lax.ppermute(lax.slice_in_dim(block, 0, width, axis=dim), axis, backward)
        block = jnp.concatenate([low, block, high], axis=dim)
    return block


def lookup(codes, table):
    result = jnp.zeros(codes.shape, jnp.float32)
    for material_no in range(3):
        result = result + jnp.where(codes == material_no, table[material_no], 0.0)
    return result


def centre(padded):
    return padded[..., 1:-1, 1:-1]


def x_plus(padded):
    return padded[..., 2:, 1:-1] - padded[..., 1:-1, 1:-1]


def x_minus(padded):
    return padded[..., 1:-1, 1:-1] - padded[..., :-2, 1:-1]


def y_plus(padded):
    return padded[..., 1:-1, 2:] - padded[..., 1:-1, 1:-1]


def y_minus(padded):
    return padded[..., 1:-1, 1:-1] - padded[..., 1:-1, :-2]


def z_plus(inner):
    upper = jnp.concatenate([inner[1:], jnp.zeros_like(inner[:1])], axis=0)
    return upper - inner


def z_minus(inner):
    lower = jnp.concatenate([jnp.zeros_like(inner[:1]), inner[:-1]], axis=0)
    return inner - lower


def advance_velocity(stress_pad, veloc, buoy_field):
    new_x = veloc[0] + buoy_field * (
        x_plus(stress_pad[0]) + y_minus(stress_pad[3]) + z_minus(centre(stress_pad[4]))
    )
    new_y = veloc[1] + buoy_field * (
        x_minus(stress_pad[3]) + y_plus(stress_pad[1]) + z_minus(centre(stress_pad[5]))
    )
    new_z = veloc[2] + buoy_field * (
        x_minus(stress_pad[4]) + y_minus(stress_pad[5]) + z_plus(centre(stress_pad[2]))
    )
    return jnp.stack([new_x, new_y, new_z])


def advance_stress(stress, veloc_pad, lame_field, shear_field):
    strain_x = x_minus(veloc_pad[0])
    strain_y = y_minus(veloc_pad[1])
    strain_z = z_minus(centre(veloc_pad[2]))
    diverge = strain_x + strain_y + strain_z
    new_xx = stress[0] + lame_field * diverge + 2.0 * shear_field * strain_x
    new_yy = stress[1] + lame_field * diverge + 2.0 * shear_field * strain_y
    new_zz = stress[2] + lame_field * diverge + 2.0 * shear_field * strain_z
    new_xy = stress[3] + shear_field * (y_plus(veloc_pad[0]) + x_plus(veloc_pad[1]))
    new_xz = stress[4] + shear_field * (z_plus(centre(veloc_pad[0])) + x_plus(veloc_pad[2]))
    new_yz = stress[5] + shear_field * (z_plus(centre(veloc_pad[1])) + y_plus(veloc_pad[2]))
    return jnp.stack([new_xx, new_yy, new_zz, new_xy, new_xz, new_yz])


def couplings(layer_kind, permit_lateral, permit_normal):
    lateral = lookup(layer_kind, permit_lateral)
    normal = lookup(layer_kind, permit_normal)
    couple = jnp.concatenate([normal[:1], 0.5 * (normal[:-1] + normal[1:]), normal[-1:]])
    return (lateral, couple)


def solve_layers(rhs, wave, lateral, couple):
    layers = rhs.shape[1]
    factors = []
    carries = []
    for layer_no in range(layers):
        pivot = couple[layer_no] + couple[layer_no + 1] + wave * lateral[layer_no]
        if layer_no > 0:
            pivot = pivot - couple[layer_no] * factors[-1]
            carry = (rhs[:, layer_no] + couple[layer_no] * carries[-1]) / pivot
        else:
            carry = rhs[:, layer_no] / pivot
        factors.append(couple[layer_no + 1] / pivot)
        carries.append(carry)
    solved = [carries[-1]]
    for layer_no in range(layers - 2, -1, -1):
        solved.append(carries[layer_no] + factors[layer_no] * solved[-1])
    return jnp.stack(solved[::-1], axis=1)


def phase_table(first, second, length):
    product = first[:, None] * second[None, :] % length
    angle = product.astype(jnp.float32) * (2.0 * math.pi / length)
    scale = 1.0 / math.sqrt(length)
    return (jnp.cos(angle) * scale, jnp.sin(angle) * scale)


def per_device(
    stress,
    velocity,
    material,
    layer_kind,
    buoyancy,
    lame_first,
    shear_modulus,
    piezo,
    permit_lateral,
    permit_normal,
):
    buoy_field = lookup(material, buoyancy)
    lame_field = lookup(material, lame_first)
    shear_field = lookup(material, shear_modulus)
    stress_pad = extended(stress, (("gx", 2), ("gy", 3)), 1)
    velocity_next = advance_velocity(stress_pad, velocity, buoy_field)
    veloc_pad = extended(velocity_next, (("gx", 2), ("gy", 3)), 1)
    stress_next = advance_stress(stress, veloc_pad, lame_field, shear_field)
    charge = lookup(material, piezo) * (stress_next[4] + stress_next[5])
    count_x = lax.axis_size("gx")
    count_y = lax.axis_size("gy")
    cells_x = charge.shape[1]
    total_x = cells_x * count_x
    total_y = charge.shape[2] * count_y
    piece = cells_x // count_y
    block_y = total_y // (count_x * count_y)
    places_x = jnp.arange(total_x, dtype=jnp.int32)
    places_y = jnp.arange(total_y, dtype=jnp.int32)
    columns = lax.all_to_all(charge, "gy", split_axis=1, concat_axis=2, tiled=True)
    true_x = (
        places_x // piece % count_x * cells_x
        + places_x // (count_x * piece) * piece
        + places_x % piece
    )
    cos_y, sin_y = phase_table(places_y, places_y, total_y)
    real_y = jnp.einsum("zxy,yk->zxk", columns, cos_y, precision=lax.Precision.HIGHEST)
    imag_y = -jnp.einsum("zxy,yk->zxk", columns, sin_y, precision=lax.Precision.HIGHEST)
    partial_value = jnp.stack([real_y, imag_y])
    lines = lax.all_to_all(
        lax.all_to_all(partial_value, "gx", split_axis=3, concat_axis=2, tiled=True),
        "gy",
        split_axis=3,
        concat_axis=2,
        tiled=True,
    )
    cos_x, sin_x = phase_table(true_x, places_x, total_x)
    with_cos = jnp.einsum("czxk,xm->czkm", lines, cos_x, precision=lax.Precision.HIGHEST)
    with_sin = jnp.einsum("czxk,xm->czkm", lines, sin_x, precision=lax.Precision.HIGHEST)
    rhs = jnp.stack([with_cos[0] + with_sin[1], with_cos[1] - with_sin[0]])
    first_y = lax.axis_index(("gx", "gy")) * block_y
    mode_y = (first_y + jnp.arange(block_y, dtype=jnp.int32)).astype(jnp.float32)
    wave_x = 2.0 * jnp.sin(math.pi * places_x.astype(jnp.float32) / total_x)
    wave_y = 2.0 * jnp.sin(math.pi * mode_y / total_y)
    wave = wave_y[:, None] * wave_y[:, None] + wave_x[None, :] * wave_x[None, :]
    lateral, couple = couplings(layer_kind, permit_lateral, permit_normal)
    potential_modes = solve_layers(rhs, wave, lateral, couple)
    return (stress_next, velocity_next, potential_modes)


def solution(mesh):
    in_specs = (
        P(None, None, "gx", "gy"),
        P(None, None, "gx", "gy"),
        P(None, "gx", "gy"),
        P(),
        P(),
        P(),
        P(),
        P(),
        P(),
        P(),
    )
    out_specs = (
        P(None, None, "gx", "gy"),
        P(None, None, "gx", "gy"),
        P(None, None, ("gx", "gy"), None),
    )
    return jax.shard_map(
        per_device, mesh=mesh, in_specs=in_specs, out_specs=out_specs, check_vma=False
    )
```

profile of v0, /device:TPU:0, one launch (start us, length us, event | category | flops | bytes accessed | tf_op | source)
XLA Modules:
  0.0 549.8 jit_solution(12410623691348603582)
XLA Ops:
  3.3 3.0 collective-permute-start
  9.1 4.4 fusion.166
  23.8 8.7 %fusion.131 = f32[16,512]{1,0:T(8,128)} fusion(f32[]{:T(128)} %bitcast.75, f32[]{:T(128)S(6)} %add.1763, f32[]{:T(128)} %bitcast.72, f32[512]{0:T(512)S(1)} %multiply_multiply_fusion, f32[16]{0:T(128)S(1)} %multiply_multiply_fusion.1, f32[]{:T(128)} %bitcast.63, f32[]{:T(128)S(6)} %add.1731, f32[]{:T(128)} %bitcast.59, f32[]{:T(128)} %bitcast.65, ...), kind=kLoop, calls=%fused_computation.260 | loop fusion | flops 270336 | bytes 34960 | tf_op jit(solution)/shard_map/sub | solution.py:100
  32.5 9.4 %broadcast_divide_fusion.8 = f32[16,512]{1,0:T(8,128)} fusion(f32[]{:T(128)} %bitcast.74, f32[]{:T(128)} %bitcast.63, f32[]{:T(128)S(6)} %add.1731, f32[]{:T(128)} %bitcast.59, f32[]{:T(128)} %bitcast.65, f32[]{:T(128)S(6)} %add.1743, f32[]{:T(128)} %bitcast.64, f32[]{:T(128)} %bitcast.67, f32[]{:T(128)S(6)} %add.1747, f32[]{:T(128)} %bitcast.66, ...), kind=kLoop, calls=%fused_computation.292 | loop fusion | flops 278528 | bytes 34964 | tf_op jit(solution)/shard_map/div | solution.py:104
  41.9 8.2 %broadcast_divide_fusion.9 = f32[16,512]{1,0:T(8,128)} fusion(f32[]{:T(128)} %bitcast.72, f32[]{:T(128)} %bitcast.63, f32[]{:T(128)S(6)} %add.1731, f32[]{:T(128)} %bitcast.59, f32[]{:T(128)} %bitcast.65, f32[]{:T(128)S(6)} %add.1743, f32[]{:T(128)} %bitcast.64, f32[]{:T(128)} %bitcast.67, f32[]{:T(128)S(6)} %add.1747, f32[]{:T(128)} %bitcast.66, ...), kind=kLoop, calls=%fused_computation.293 | loop fusion | flops 237568 | bytes 34952 | tf_op jit(solution)/shard_map/div | solution.py:104
  52.5 10.1 %fusion.133 = f32[16,512]{1,0:T(8,128)} fusion(f32[]{:T(128)} %bitcast.77, f32[]{:T(128)S(6)} %add.1767, f32[]{:T(128)} %bitcast.74, f32[512]{0:T(512)S(1)} %multiply_multiply_fusion, f32[16]{0:T(128)S(1)} %multiply_multiply_fusion.1, f32[]{:T(128)} %bitcast.63, f32[]{:T(128)S(6)} %add.1731, f32[]{:T(128)} %bitcast.59, f32[]{:T(128)} %bitcast.65, ...), kind=kLoop, calls=%fused_computation.262 | loop fusion | flops 311296 | bytes 34972 | tf_op jit(solution)/shard_map/sub | solution.py:100
  62.6 11.3 %fusion.135 = f32[16,512]{1,0:T(8,128)} fusion(f32[]{:T(128)} %bitcast.79, f32[]{:T(128)S(6)} %add.1771, f32[]{:T(128)} %bitcast.76, f32[512]{0:T(512)S(1)} %multiply_multiply_fusion, f32[16]{0:T(128)S(1)} %multiply_multiply_fusion.1, f32[]{:T(128)} %bitcast.63, f32[]{:T(128)S(6)} %add.1731, f32[]{:T(128)} %bitcast.59, f32[]{:T(128)} %bitcast.65, ...), kind=kLoop, calls=%fused_computation.264 | loop fusion | flops 352256 | bytes 34984 | tf_op jit(solution)/shard_map/sub | solution.py:100
  73.9 11.9 %broadcast_divide_fusion.6 = f32[16,512]{1,0:T(8,128)} fusion(f32[]{:T(128)} %bitcast.78, f32[]{:T(128)} %bitcast.63, f32[]{:T(128)S(6)} %add.1731, f32[]{:T(128)} %bitcast.59, f32[]{:T(128)} %bitcast.65, f32[]{:T(128)S(6)} %add.1743, f32[]{:T(128)} %bitcast.64, f32[]{:T(128)} %bitcast.67, f32[]{:T(128)S(6)} %add.1747, f32[]{:T(128)} %bitcast.66, ...), kind=kLoop, calls=%fused_computation.290 | loop fusion | flops 360448 | bytes 34988 | tf_op jit(solution)/shard_map/div | solution.py:104
  85.9 10.7 %broadcast_divide_fusion.7 = f32[16,512]{1,0:T(8,128)} fusion(f32[]{:T(128)} %bitcast.76, f32[]{:T(128)} %bitcast.63, f32[]{:T(128)S(6)} %add.1731, f32[]{:T(128)} %bitcast.59, f32[]{:T(128)} %bitcast.65, f32[]{:T(128)S(6)} %add.1743, f32[]{:T(128)} %bitcast.64, f32[]{:T(128)} %bitcast.67, f32[]{:T(128)S(6)} %add.1747, f32[]{:T(128)} %bitcast.66, ...), kind=kLoop, calls=%fused_computation.291 | loop fusion | flops 319488 | bytes 34976 | tf_op jit(solution)/shard_map/div | solution.py:104
  98.8 12.6 %fusion.137 = f32[16,512]{1,0:T(8,128)} fusion(f32[]{:T(128)} %bitcast.81, f32[]{:T(128)S(6)} %add.1775, f32[]{:T(128)} %bitcast.78, f32[512]{0:T(512)S(1)} %multiply_multiply_fusion, f32[16]{0:T(128)S(1)} %multiply_multiply_fusion.1, f32[]{:T(128)} %bitcast.63, f32[]{:T(128)S(6)} %add.1731, f32[]{:T(128)} %bitcast.59, f32[]{:T(128)} %bitcast.65, ...), kind=kLoop, calls=%fused_computation.266 | loop fusion | flops 393216 | bytes 34996 | tf_op jit(solution)/shard_map/sub | solution.py:100
  111.5 13.8 %fusion.139 = f32[16,512]{1,0:T(8,128)} fusion(f32[]{:T(128)} %bitcast.83, f32[]{:T(128)S(6)} %add.1779, f32[]{:T(128)} %bitcast.80, f32[512]{0:T(512)S(1)} %multiply_multiply_fusion, f32[16]{0:T(128)S(1)} %multiply_multiply_fusion.1, f32[]{:T(128)} %bitcast.63, f32[]{:T(128)S(6)} %add.1731, f32[]{:T(128)} %bitcast.59, f32[]{:T(128)} %bitcast.65, ...), kind=kLoop, calls=%fused_computation.268 | loop fusion | flops 434176 | bytes 35008 | tf_op jit(solution)/shard_map/sub | solution.py:100
  125.3 14.4 %broadcast_divide_fusion.4 = f32[16,512]{1,0:T(8,128)} fusion(f32[]{:T(128)} %bitcast.82, f32[]{:T(128)} %bitcast.63, f32[]{:T(128)S(6)} %add.1731, f32[]{:T(128)} %bitcast.59, f32[]{:T(128)} %bitcast.65, f32[]{:T(128)S(6)} %add.1743, f32[]{:T(128)} %bitcast.64, f32[]{:T(128)} %bitcast.67, f32[]{:T(128)S(6)} %add.1747, f32[]{:T(128)} %bitcast.66, ...), kind=kLoop, calls=%fused_computation.288 | loop fusion | flops 442368 | bytes 35012 | tf_op jit(solution)/shard_map/div | solution.py:104
  139.7 13.2 %broadcast_divide_fusion.5 = f32[16,512]{1,0:T(8,128)} fusion(f32[]{:T(128)} %bitcast.80, f32[]{:T(128)} %bitcast.63, f32[]{:T(128)S(6)} %add.1731, f32[]{:T(128)} %bitcast.59, f32[]{:T(128)} %bitcast.65, f32[]{:T(128)S(6)} %add.1743, f32[]{:T(128)} %bitcast.64, f32[]{:T(128)} %bitcast.67, f32[]{:T(128)S(6)} %add.1747, f32[]{:T(128)} %bitcast.66, ...), kind=kLoop, calls=%fused_computation.289 | loop fusion | flops 401408 | bytes 35000 | tf_op jit(solution)/shard_map/div | solution.py:104
  155.4 15.0 %fusion.141 = f32[16,512]{1,0:T(8,128)} fusion(f32[]{:T(128)} %bitcast.85, f32[]{:T(128)S(6)} %add.1783, f32[]{:T(128)} %bitcast.82, f32[512]{0:T(512)S(1)} %multiply_multiply_fusion, f32[16]{0:T(128)S(1)} %multiply_multiply_fusion.1, f32[]{:T(128)} %bitcast.63, f32[]{:T(128)S(6)} %add.1731, f32[]{:T(128)} %bitcast.59, f32[]{:T(128)} %bitcast.65, ...), kind=kLoop, calls=%fused_computation.270 | loop fusion | flops 475136 | bytes 35020 | tf_op jit(solution)/shard_map/sub | solution.py:100
  170.3 16.3 %fusion.143 = f32[16,512]{1,0:T(8,128)} fusion(f32[]{:T(128)} %bitcast.87, f32[]{:T(128)S(6)} %add.1787, f32[]{:T(128)} %bitcast.84, f32[512]{0:T(512)S(1)} %multiply_multiply_fusion, f32[16]{0:T(128)S(1)} %multiply_multiply_fusion.1, f32[]{:T(128)} %bitcast.63, f32[]{:T(128)S(6)} %add.1731, f32[]{:T(128)} %bitcast.59, f32[]{:T(128)} %bitcast.65, ...), kind=kLoop, calls=%fused_computation.272 | loop fusion | flops 516096 | bytes 35032 | tf_op jit(solution)/shard_map/sub | solution.py:100
  186.6 16.2 %broadcast_divide_fusion.2 = f32[16,512]{1,0:T(8,128)S(1)} fusion(f32[]{:T(128)} %bitcast.86, f32[]{:T(128)} %bitcast.63, f32[]{:T(128)S(6)} %add.1731, f32[]{:T(128)} %bitcast.59, f32[]{:T(128)} %bitcast.65, f32[]{:T(128)S(6)} %add.1743, f32[]{:T(128)} %bitcast.64, f32[]{:T(128)} %bitcast.67, f32[]{:T(128)S(6)} %add.1747, f32[]{:T(128)} %bitcast.66, ...), kind=kLoop, calls=%fused_computation.286 | loop fusion | flops 524288 | bytes 35036 | tf_op jit(solution)/shard_map/div | solution.py:104
  202.8 15.7 %broadcast_divide_fusion.3 = f32[16,512]{1,0:T(8,128)} fusion(f32[]{:T(128)} %bitcast.84, f32[]{:T(128)} %bitcast.63, f32[]{:T(128)S(6)} %add.1731, f32[]{:T(128)} %bitcast.59, f32[]{:T(128)} %bitcast.65, f32[]{:T(128)S(6)} %add.1743, f32[]{:T(128)} %bitcast.64, f32[]{:T(128)} %bitcast.67, f32[]{:T(128)S(6)} %add.1747, f32[]{:T(128)} %bitcast.66, ...), kind=kLoop, calls=%fused_computation.287 | loop fusion | flops 483328 | bytes 35024 | tf_op jit(solution)/shard_map/div | solution.py:104
  218.5 2.5 fusion.205
  222.1 17.6 %fusion.145 = f32[16,512]{1,0:T(8,128)} fusion(f32[]{:T(128)} %bitcast.89, f32[]{:T(128)S(6)} %add.1791, f32[]{:T(128)} %bitcast.86, f32[512]{0:T(512)S(1)} %multiply_multiply_fusion, f32[16]{0:T(128)S(1)} %multiply_multiply_fusion.1, f32[]{:T(128)} %bitcast.63, f32[]{:T(128)S(6)} %add.1731, f32[]{:T(128)} %bitcast.59, f32[]{:T(128)} %bitcast.65, ...), kind=kLoop, calls=%fused_computation.274 | loop fusion | flops 557056 | bytes 35044 | tf_op jit(solution)/shard_map/sub | solution.py:100
  240.3 4.3 copy.42
  244.6 4.2 copy.51
  248.8 4.2 copy.49
  255.6 5.7 %collective-permute-start.2 = (f32[6,16,66,1]{2,1,3,0:T(8,128)S(1)}, f32[6,16,66,1]{2,1,3,0:T(8,128)S(1)}, u32[]{:S(2)}, u32[]{:S(2)}) collective-permute-start(f32[6,16,66,1]{2,1,3,0:T(8,128)S(1)} %get-tuple-element.41), channel_id=1, source_target_pairs={{0,1},{1,2},{2,3},{4,5},{5,6},{6,7},{8,9},{9,10},{10,11},{12,13},{... | collective-permute-start | bytes 76040 | tf_op jit(solution)/shard_map/ppermute | solution.py:14
  265.7 8.2 %pad_maximum_fusion = f32[6,16,66,130]{2,1,3,0:T(8,128)S(1)} fusion(f32[6,16,66,1]{2,1,3,0:T(8,128)S(1)} %collective-permute-done.3, f32[6,16,1,128]{2,1,3,0:T(8,128)} %copy.51, f32[6,16,64,128]{2,1,3,0:T(8,128)} %copy.42, f32[6,16,1,128]{2,1,3,0:T(8,128)} %copy.49, f32[6,16,66,1]{2,1,3,0:T(8,128)S(1)} %collective-permute-done.2), kind=kLoop, calls=%fused_computation | loop fusion | flops 3294720 | bytes 6589440 | tf_op jit(solution)/shard_map/concatenate | solution.py:18
  276.0 3.3 fusion.40
  279.4 3.1 fusion.29
  282.5 3.1 fusion.35
  286.8 2.7 fusion.203
  289.5 2.4 copy.55
  294.4 3.5 collective-permute-start.4
  299.8 2.2 copy.56
  304.3 5.0 collective-permute-start.6
  312.5 4.3 pad_maximum_fusion.1
  318.1 8.3 %add_multiply_fusion = (f32[16,64,128]{1,0,2:T(8,128)}, f32[16,64,128]{1,0,2:T(8,128)}, f32[16,64,128]{1,0,2:T(8,128)}) fusion(pred[16,64,128]{1,0,2:T(8,128)(4,1)S(1)} %copy-done.8, pred[16,64,128]{1,0,2:T(8,128)(4,1)S(1)} %copy-done.5, pred[16,64,128]{1,0,2:T(8,128)(4,1)S(1)} %get-tuple-element.38, f32[]{:T(128)} %bitcast.38, f32[]{:T(128)} %bitcast.37, ...), kind=kLoop, calls=%fused_computation.135 | loop fusion | flops 2883584 | bytes 6619160 | tf_op jit(solution)/shard_map/mul | solution.py:138
  326.4 2.5 copy.63
  328.9 4.1 all-to-all-start
  333.1 18.1 %broadcast_divide_fusion.1 = f32[16,512]{1,0:T(8,128)} fusion(f32[]{:T(128)} %bitcast.88, f32[]{:T(128)} %bitcast.63, f32[]{:T(128)S(6)} %add.1731, f32[]{:T(128)} %bitcast.59, f32[]{:T(128)} %bitcast.65, f32[]{:T(128)S(6)} %add.1743, f32[]{:T(128)} %bitcast.64, f32[]{:T(128)} %bitcast.67, f32[]{:T(128)S(6)} %add.1747, f32[]{:T(128)} %bitcast.66, ...), kind=kLoop, calls=%fused_computation.285 | loop fusion | flops 565248 | bytes 35048 | tf_op jit(solution)/shard_map/div | solution.py:104
  351.2 19.4 %broadcast_divide_fusion = f32[16,512]{1,0:T(8,128)} fusion(f32[]{:T(128)} %bitcast.90, f32[]{:T(128)} %bitcast.63, f32[]{:T(128)S(6)} %add.1731, f32[]{:T(128)} %bitcast.59, f32[]{:T(128)} %bitcast.65, f32[]{:T(128)S(6)} %add.1743, f32[]{:T(128)} %bitcast.64, f32[]{:T(128)} %bitcast.67, f32[]{:T(128)S(6)} %add.1747, f32[]{:T(128)} %bitcast.66, ...), kind=kLoop, calls=%fused_computation.284 | loop fusion | flops 606208 | bytes 35060 | tf_op jit(solution)/shard_map/div | solution.py:104
  370.5 18.7 %fusion.147 = f32[16,512]{1,0:T(8,128)} fusion(f32[]{:T(128)} %bitcast.91, f32[]{:T(128)S(6)} %add.1795, f32[]{:T(128)} %bitcast.88, f32[512]{0:T(512)S(1)} %multiply_multiply_fusion, f32[16]{0:T(128)S(1)} %multiply_multiply_fusion.1, f32[]{:T(128)} %bitcast.63, f32[]{:T(128)S(6)} %add.1731, f32[]{:T(128)} %bitcast.59, f32[]{:T(128)} %bitcast.65, ...), kind=kLoop, calls=%fused_computation.276 | loop fusion | flops 598016 | bytes 35056 | tf_op jit(solution)/shard_map/sub | solution.py:100
  389.3 2.2 copy.81
  391.4 2.0 all_to_all.42
  393.5 6.4 %fusion = f32[1,16,16,512]{3,2,1,0:T(8,128)S(1)} fusion(f32[16,16,512]{2,1,0:T(8,128)} %all_to_all.42), kind=kOutput, calls=%fused_computation.40 | convolution fusion | flops 809369600 | bytes 1048576 | tf_op jit(solution)/shard_map/zxy,yk->zxk/dot_general | solution.py:156
  399.9 5.3 convolution_bitcast_fusion
  406.3 8.3 %copy.65 = f32[2,16,16,512]{2,1,0,3:T(8,128)} copy(f32[2,16,16,512]{3,2,1,0:T(8,128)} %pad_maximum_fusion.3) | data formatting | bytes 2097152 | tf_op jit(solution)/shard_map/stack | solution.py:157
  414.7 8.1 %reshape.956 = f32[8,1,32768]{2,1,0:T(1,128)} reshape(f32[512,2,16,16]{3,2,1,0:T(8,128)} %bitcast.187) | data formatting | bytes 2097152
  422.8 7.1 %all-to-all-start.1 = ((f32[8,1,32768]{2,1,0:T(1,128)}), f32[8,1,32768]{2,1,0:T(1,128)}, u32[]{:S(2)}, u32[]{:S(2)}) async-start(f32[8,1,32768]{2,1,0:T(1,128)} %reshape.956), calls=%async_computation.1 | async-start | bytes 2097152 | tf_op jit(solution)/shard_map/all_to_all | solution.py:159
  429.9 20.0 %fusion.149 = f32[16,512]{1,0:T(8,128)} fusion(f32[]{:T(128)} %bitcast.93, f32[]{:T(128)S(6)} %add.1799, f32[]{:T(128)} %bitcast.90, f32[512]{0:T(512)S(1)} %multiply_multiply_fusion, f32[16]{0:T(128)S(1)} %multiply_multiply_fusion.1, f32[]{:T(128)} %bitcast.63, f32[]{:T(128)S(6)} %add.1731, f32[]{:T(128)} %bitcast.59, f32[]{:T(128)} %bitcast.65, ...), kind=kLoop, calls=%fused_computation.278 | loop fusion | flops 638976 | bytes 35068 | tf_op jit(solution)/shard_map/sub | solution.py:100
  449.9 7.6 %broadcast_divide_fusion.11 = (f32[16,512]{1,0:T(8,128)}, f32[16,512]{1,0:T(8,128)}, f32[16,512]{1,0:T(8,128)}, f32[16,512]{1,0:T(8,128)}, f32[16,512]{1,0:T(8,1...) fusion(f32[]{:T(128)} %bitcast.68, f32[]{:T(128)} %bitcast.63, ...), kind=kLoop, calls=%fused_computation.295 | loop fusion | flops 229376 | bytes 362628 | tf_op jit(solution)/shard_map/div | solution.py:104
  457.6 3.2 copy.71
  462.2 7.5 %fusion.44 = (f32[6,16,64,128]{2,1,3,0:T(8,128)}, f32[16,64,128]{1,0,2:T(8,128)}) fusion(f32[6,16,64,128]{2,1,3,0:T(8,128)} %copy.42, f32[16,66,130]{1,0,2:T(8,128)S(1)} %get-tuple-element.53, pred[16,64,128]{1,0,2:T(8,128)(4,1)} %copy-done.7, f32[]{:T(128)} %bitcast.24, pred[16,64,128]{1,0,2:T(8,128)(4,1)} %copy-done.4, f32[]{:T(128)} %bitcast.23, ...), kind=kLoop, calls=%fused_computation.113 | loop fusion | flops 2621439 | bytes 6127640
  470.3 5.3 reduce
  475.6 7.4 %reshape.957 = f32[512,2,16,16]{3,2,1,0:T(8,128)} reshape(f32[8,32768]{1,0:T(8,128)} %reduce) | data formatting | bytes 2097152
  482.9 6.3 %copy.66 = f32[2,16,16,8,64]{4,2,3,1,0:T(8,128)} copy(f32[2,16,16,8,64]{2,1,0,4,3:T(8,128)} %bitcast.186) | data formatting | bytes 2097152 | tf_op jit(solution)/shard_map/all_to_all | solution.py:159
  489.2 3.4 copy.67
  492.6 5.0 all-to-all-start.2
  497.7 5.3 fusion.25
  503.0 4.7 fusion.21
  507.7 5.4 fusion.17
  515.2 6.5 %copy.70 = f32[6,16,64,128]{3,2,1,0:T(8,128)} copy(f32[6,16,64,128]{2,1,3,0:T(8,128)} %bitcast_dynamic-update-slice_fusion) | data formatting | bytes 6291456
  521.8 2.4 all-to-all-done.2
  524.2 1.9 copy.69
  526.5 5.8 %fusion.45 = f32[2,16,16,512]{3,2,1,0:T(8,128)S(1)} fusion(f32[2,16,512,16]{2,3,1,0:T(8,128)S(1)} %all_to_all.50, s32[512]{0:T(512)S(1)} %fusion.157), kind=kOutput, calls=%fused_computation.115 | convolution fusion | flops 1614544896 | bytes 2099200 | tf_op jit(solution)/shard_map/czxk,xm->czkm/dot_general | solution.py:167
  532.4 5.8 %fusion.47 = f32[2,16,16,512]{3,2,1,0:T(8,128)S(1)} fusion(f32[2,16,512,16]{2,3,1,0:T(8,128)S(1)} %all_to_all.50, s32[512]{0:T(512)S(1)} %fusion.157), kind=kOutput, calls=%fused_computation.117 | convolution fusion | flops 1614544896 | bytes 2099200 | tf_op jit(solution)/shard_map/czxk,xm->czkm/dot_general | solution.py:166
  538.8 8.0 %fusion.118 = (f32[2,1,16,512]{3,2,1,0:T(8,128)S(1)}, f32[2,1,16,512]{3,2,1,0:T(8,128)S(1)}, f32[2,1,16,512]{3,2,1,0:T(8,128)S(1)}, f32[2,1,16,512]{3,2,1,0:T(8,...) fusion(f32[1,16,16,512]{3,2,1,0:T(8,128)S(1)} %get-tuple-elemen, ...), kind=kLoop, calls=%fused_computation.229 | loop fusion | flops 884736 | bytes 2359348 | tf_op jit(solution)/shard_map/div | solution.py:101
  (180 shorter events, 34.7 us)
Async XLA Ops:
  0.6 239.7 %copy-start.17 = (f32[6,16,64,128]{3,2,1,0:T(8,128)S(1)}, f32[6,16,64,128]{3,2,1,0:T(8,128)}, u32[]{:S(2)}) copy-start(f32[6,16,64,128]{3,2,1,0:T(8,128)} %param.10) | copy-start | bytes 9437188
  0.6 239.0 %copy-start.52 = (f32[3]{0:T(128)S(1)}, f32[3]{0:T(128)}, u32[]{:S(2)}) copy-start(f32[3]{0:T(128)} %param.14) | copy-start | bytes 40
  2.0 242.6 %collective-permute-start.1 = (f32[6,16,1,128]{3,1,2,0:T(8,128)S(1)}, f32[6,16,1,128]{3,1,2,0:T(8,128)S(1)}, u32[]{:S(2)}, u32[]{:S(2)}) collective-permute-start(f32[6,16,1,128]{3,1,2,0:T(8,128)S(1)} %bitcast.191), channel_id=1, source_target_pairs={{4,0},{8,4},{12,8},{16,12},{20,16},{24,20},{28,24},{5,1},{9,5},{13... | collective-permute-start | bytes 147464 | tf_op jit(solution)/shard_map/ppermute | solution.py:17
  3.3 245.5 %collective-permute-start = (f32[6,16,1,128]{3,1,2,0:T(8,128)S(1)}, f32[6,16,1,128]{3,1,2,0:T(8,128)S(1)}, u32[]{:S(2)}, u32[]{:S(2)}) collective-permute-start(f32[6,16,1,128]{3,1,2,0:T(8,128)S(1)} %bitcast.190), channel_id=1, source_target_pairs={{0,4},{4,8},{8,12},{12,16},{16,20},{20,24},{24,28},{1,5},{5,9},{9,... | collective-permute-start | bytes 147464 | tf_op jit(solution)/shard_map/ppermute | solution.py:14
  253.0 8.3 %copy-start.53 = (f32[3]{0:T(128)S(1)}, f32[3]{0:T(128)}, u32[]{:S(2)}) copy-start(f32[3]{0:T(128)} %param.16) | copy-start | bytes 40
  253.0 8.9 %copy-start.20 = (f32[1,16,64,128]{3,2,1,0:T(8,128)S(1)}, f32[1,16,64,128]{3,2,1,0:T(8,128)}, u32[]{:S(2)}) copy-start(f32[1,16,64,128]{3,2,1,0:T(8,128)} %get-tuple-element.62) | copy-start | bytes 1572868
  253.0 9.5 %copy-start.19 = (f32[1,16,64,128]{3,2,1,0:T(8,128)S(1)}, f32[1,16,64,128]{3,2,1,0:T(8,128)}, u32[]{:S(2)}) copy-start(f32[1,16,64,128]{3,2,1,0:T(8,128)} %get-tuple-element.61) | copy-start | bytes 1572868
  254.1 9.7 %copy-start.21 = (s32[16,64,128]{2,1,0:T(8,128)S(1)}, s32[16,64,128]{2,1,0:T(8,128)}, u32[]{:S(2)}) copy-start(s32[16,64,128]{2,1,0:T(8,128)} %param.12) | copy-start | bytes 1572868
  254.1 11.1 %copy-start.18 = (f32[1,16,64,128]{3,2,1,0:T(8,128)S(1)}, f32[1,16,64,128]{3,2,1,0:T(8,128)}, u32[]{:S(2)}) copy-start(f32[1,16,64,128]{3,2,1,0:T(8,128)} %get-tuple-element.60) | copy-start | bytes 1572868
  254.2 11.6 %collective-permute-start.3 = (f32[6,16,66,1]{2,1,3,0:T(8,128)S(1)}, f32[6,16,66,1]{2,1,3,0:T(8,128)S(1)}, u32[]{:S(2)}, u32[]{:S(2)}) collective-permute-start(f32[6,16,66,1]{2,1,3,0:T(8,128)S(1)} %get-tuple-element.42), channel_id=1, source_target_pairs={{1,0},{2,1},{3,2},{5,4},{6,5},{7,6},{9,8},{10,9},{11,10},{13,12},{... | collective-permute-start | bytes 76040 | tf_op jit(solution)/shard_map/ppermute | solution.py:17
  255.6 10.1 %collective-permute-start.2 = (f32[6,16,66,1]{2,1,3,0:T(8,128)S(1)}, f32[6,16,66,1]{2,1,3,0:T(8,128)S(1)}, u32[]{:S(2)}, u32[]{:S(2)}) collective-permute-start(f32[6,16,66,1]{2,1,3,0:T(8,128)S(1)} %get-tuple-element.41), channel_id=1, source_target_pairs={{0,1},{1,2},{2,3},{4,5},{5,6},{6,7},{8,9},{9,10},{10,11},{12,13},{... | collective-permute-start | bytes 76040 | tf_op jit(solution)/shard_map/ppermute | solution.py:14
  274.5 1.2 copy-start.15
  274.5 1.5 copy-start.16
  279.3 3.1 copy-start.4
  279.3 3.1 copy-start.7
  279.4 6.2 %copy-start.3 = (f32[1,16,64,128]{2,1,3,0:T(8,128)}, f32[1,16,64,128]{2,1,3,0:T(8,128)S(1)}, u32[]{:S(2)}) copy-start(f32[1,16,64,128]{2,1,3,0:T(8,128)S(1)} %get-tuple-element.37) | copy-start | bytes 1572868
  282.4 3.1 copy-start.1
  286.8 2.8 copy-start
  289.5 8.4 %copy-start.54 = (f32[3]{0:T(128)S(1)}, f32[3]{0:T(128)}, u32[]{:S(2)}) copy-start(f32[3]{0:T(128)} %param.15) | copy-start | bytes 40
  291.9 6.7 %collective-permute-start.5 = (f32[3,16,1,128]{3,1,2,0:T(8,128)S(1)}, f32[3,16,1,128]{3,1,2,0:T(8,128)S(1)}, u32[]{:S(2)}, u32[]{:S(2)}) collective-permute-start(f32[3,16,1,128]{3,1,2,0:T(8,128)S(1)} %copy.55), channel_id=1, source_target_pairs={{4,0},{8,4},{12,8},{16,12},{20,16},{24,20},{28,24},{5,1},{9,5},{13... | collective-permute-start | bytes 73736 | tf_op jit(solution)/shard_map/ppermute | solution.py:17
  294.4 5.4 collective-permute-start.4
  302.0 7.2 %copy-start.55 = (f32[3]{0:T(128)S(1)}, f32[3]{0:T(128)}, u32[]{:S(2)}) copy-start(f32[3]{0:T(128)} %param.17) | copy-start | bytes 40
  303.0 9.5 %collective-permute-start.7 = (f32[3,16,66,1]{2,1,3,0:T(8,128)S(1)}, f32[3,16,66,1]{2,1,3,0:T(8,128)S(1)}, u32[]{:S(2)}, u32[]{:S(2)}) collective-permute-start(f32[3,16,66,1]{2,1,3,0:T(8,128)S(1)} %get-tuple-element.44), channel_id=1, source_target_pairs={{1,0},{2,1},{3,2},{5,4},{6,5},{7,6},{9,8},{10,9},{11,10},{13,12},{... | collective-permute-start | bytes 38024 | tf_op jit(solution)/shard_map/ppermute | solution.py:17
  304.3 8.2 %collective-permute-start.6 = (f32[3,16,66,1]{2,1,3,0:T(8,128)S(1)}, f32[3,16,66,1]{2,1,3,0:T(8,128)S(1)}, u32[]{:S(2)}, u32[]{:S(2)}) collective-permute-start(f32[3,16,66,1]{2,1,3,0:T(8,128)S(1)} %get-tuple-element.43), channel_id=1, source_target_pairs={{0,1},{1,2},{2,3},{4,5},{5,6},{6,7},{8,9},{9,10},{10,11},{12,13},{... | collective-permute-start | bytes 38024 | tf_op jit(solution)/shard_map/ppermute | solution.py:14
  328.9 60.3 %all-to-all-start = ((f32[16,64,128]{2,0,1:T(8,128)}), f32[16,64,128]{2,0,1:T(8,128)}, u32[]{:S(2)}, u32[]{:S(2)}) async-start(f32[16,64,128]{2,0,1:T(8,128)} %copy.63), calls=%async_computation | async-start | bytes 1048576 | tf_op jit(solution)/shard_map/all_to_all | solution.py:148
  393.5 6.4 %copy-start.22 = (f32[16,16,512]{2,1,0:T(8,128)S(1)}, f32[16,16,512]{2,1,0:T(8,128)}, u32[]{:S(2)}) copy-start(f32[16,16,512]{2,1,0:T(8,128)} %all_to_all.42) | copy-start | bytes 1572868
  422.8 47.0 %all-to-all-start.1 = ((f32[8,1,32768]{2,1,0:T(1,128)}), f32[8,1,32768]{2,1,0:T(1,128)}, u32[]{:S(2)}, u32[]{:S(2)}) async-start(f32[8,1,32768]{2,1,0:T(1,128)} %reshape.956), calls=%async_computation.1 | async-start | bytes 2097152 | tf_op jit(solution)/shard_map/all_to_all | solution.py:159
  461.1 1.1 copy-start.10
  492.6 31.5 %all-to-all-start.2 = ((f32[2,16,128,64]{2,1,0,3:T(8,128)}), f32[2,16,128,64]{2,1,0,3:T(8,128)}, u32[]{:S(2)}, u32[]{:S(2)}) async-start(f32[2,16,128,64]{2,1,0,3:T(8,128)} %copy.67), calls=%async_computation.2 | async-start | bytes 2097152 | tf_op jit(solution)/shard_map/all_to_all | solution.py:158
  497.6 5.3 copy-start.6
  497.7 5.3 copy-start.9
  497.7 5.3 copy-start.11
  497.7 5.3 copy-start.12
  507.7 5.4 copy-start.14
  507.7 6.4 %copy-start.13 = (f32[16,64,128]{1,0,2:T(8,128)S(1)}, f32[16,64,128]{1,0,2:T(8,128)}, u32[]{:S(2)}) copy-start(f32[16,64,128]{1,0,2:T(8,128)} %get-tuple-element.33) | copy-start | bytes 1572868
  532.3 6.3 %copy-start.32 = (f32[16,512]{1,0:T(8,128)S(1)}, f32[16,512]{1,0:T(8,128)}, u32[]{:S(2)}) copy-start(f32[16,512]{1,0:T(8,128)} %get-tuple-element.64) | copy-start | bytes 98308
  532.3 6.3 %copy-start.33 = (f32[16,512]{1,0:T(8,128)S(1)}, f32[16,512]{1,0:T(8,128)}, u32[]{:S(2)}) copy-start(f32[16,512]{1,0:T(8,128)} %get-tuple-element.66) | copy-start | bytes 98308
  532.3 6.3 %copy-start.34 = (f32[16,512]{1,0:T(8,128)S(1)}, f32[16,512]{1,0:T(8,128)}, u32[]{:S(2)}) copy-start(f32[16,512]{1,0:T(8,128)} %get-tuple-element.68) | copy-start | bytes 98308
  532.3 6.3 %copy-start.35 = (f32[16,512]{1,0:T(8,128)S(1)}, f32[16,512]{1,0:T(8,128)}, u32[]{:S(2)}) copy-start(f32[16,512]{1,0:T(8,128)} %get-tuple-element.71) | copy-start | bytes 98308
  532.3 6.3 %copy-start.36 = (f32[16,512]{1,0:T(8,128)S(1)}, f32[16,512]{1,0:T(8,128)}, u32[]{:S(2)}) copy-start(f32[16,512]{1,0:T(8,128)} %get-tuple-element.73) | copy-start | bytes 98308
  532.3 6.3 %copy-start.37 = (f32[16,512]{1,0:T(8,128)S(1)}, f32[16,512]{1,0:T(8,128)}, u32[]{:S(2)}) copy-start(f32[16,512]{1,0:T(8,128)} %fusion.145) | copy-start | bytes 98308
  532.4 6.3 %copy-start.44 = (f32[16,512]{1,0:T(8,128)S(1)}, f32[16,512]{1,0:T(8,128)}, u32[]{:S(2)}) copy-start(f32[16,512]{1,0:T(8,128)} %fusion.131) | copy-start | bytes 98308
  532.4 6.3 %copy-start.45 = (f32[16,512]{1,0:T(8,128)S(1)}, f32[16,512]{1,0:T(8,128)}, u32[]{:S(2)}) copy-start(f32[16,512]{1,0:T(8,128)} %fusion.133) | copy-start | bytes 98308
  532.4 6.3 %copy-start.46 = (f32[16,512]{1,0:T(8,128)S(1)}, f32[16,512]{1,0:T(8,128)}, u32[]{:S(2)}) copy-start(f32[16,512]{1,0:T(8,128)} %fusion.135) | copy-start | bytes 98308
  532.4 6.3 %copy-start.47 = (f32[16,512]{1,0:T(8,128)S(1)}, f32[16,512]{1,0:T(8,128)}, u32[]{:S(2)}) copy-start(f32[16,512]{1,0:T(8,128)} %fusion.137) | copy-start | bytes 98308
  532.4 6.3 %copy-start.48 = (f32[16,512]{1,0:T(8,128)S(1)}, f32[16,512]{1,0:T(8,128)}, u32[]{:S(2)}) copy-start(f32[16,512]{1,0:T(8,128)} %fusion.139) | copy-start | bytes 98308
  532.4 6.3 %copy-start.49 = (f32[16,512]{1,0:T(8,128)S(1)}, f32[16,512]{1,0:T(8,128)}, u32[]{:S(2)}) copy-start(f32[16,512]{1,0:T(8,128)} %fusion.141) | copy-start | bytes 98308
  532.4 6.3 %copy-start.50 = (f32[16,512]{1,0:T(8,128)S(1)}, f32[16,512]{1,0:T(8,128)}, u32[]{:S(2)}) copy-start(f32[16,512]{1,0:T(8,128)} %fusion.143) | copy-start | bytes 98308
  538.2 8.6 %copy-start.23 = (f32[16,512]{1,0:T(8,128)S(1)}, f32[16,512]{1,0:T(8,128)}, u32[]{:S(2)}) copy-start(f32[16,512]{1,0:T(8,128)} %broadcast_divide_fusion) | copy-start | bytes 98308
  538.2 8.6 %copy-start.24 = (f32[16,512]{1,0:T(8,128)S(1)}, f32[16,512]{1,0:T(8,128)}, u32[]{:S(2)}) copy-start(f32[16,512]{1,0:T(8,128)} %get-tuple-element.72) | copy-start | bytes 98308
  538.2 8.6 %copy-start.25 = (f32[16,512]{1,0:T(8,128)S(1)}, f32[16,512]{1,0:T(8,128)}, u32[]{:S(2)}) copy-start(f32[16,512]{1,0:T(8,128)} %get-tuple-element.65) | copy-start | bytes 98308
  538.2 8.6 %copy-start.26 = (f32[16,512]{1,0:T(8,128)S(1)}, f32[16,512]{1,0:T(8,128)}, u32[]{:S(2)}) copy-start(f32[16,512]{1,0:T(8,128)} %broadcast_divide_fusion.4) | copy-start | bytes 98308
  538.2 8.6 %copy-start.27 = (f32[16,512]{1,0:T(8,128)S(1)}, f32[16,512]{1,0:T(8,128)}, u32[]{:S(2)}) copy-start(f32[16,512]{1,0:T(8,128)} %broadcast_divide_fusion.6) | copy-start | bytes 98308
  538.2 8.6 %copy-start.28 = (f32[16,512]{1,0:T(8,128)S(1)}, f32[16,512]{1,0:T(8,128)}, u32[]{:S(2)}) copy-start(f32[16,512]{1,0:T(8,128)} %broadcast_divide_fusion.8) | copy-start | bytes 98308
  538.3 8.6 %copy-start.29 = (f32[16,512]{1,0:T(8,128)S(1)}, f32[16,512]{1,0:T(8,128)}, u32[]{:S(2)}) copy-start(f32[16,512]{1,0:T(8,128)} %get-tuple-element.63) | copy-start | bytes 98308
  538.3 8.6 %copy-start.30 = (f32[16,512]{1,0:T(8,128)S(1)}, f32[16,512]{1,0:T(8,128)}, u32[]{:S(2)}) copy-start(f32[16,512]{1,0:T(8,128)} %get-tuple-element.67) | copy-start | bytes 98308
  538.3 8.6 %copy-start.31 = (f32[16,512]{1,0:T(8,128)S(1)}, f32[16,512]{1,0:T(8,128)}, u32[]{:S(2)}) copy-start(f32[16,512]{1,0:T(8,128)} %get-tuple-element.69) | copy-start | bytes 98308
  538.3 8.6 %copy-start.38 = (f32[16,512]{1,0:T(8,128)S(1)}, f32[16,512]{1,0:T(8,128)}, u32[]{:S(2)}) copy-start(f32[16,512]{1,0:T(8,128)} %broadcast_divide_fusion.1) | copy-start | bytes 98308
  538.3 8.6 %copy-start.39 = (f32[16,512]{1,0:T(8,128)S(1)}, f32[16,512]{1,0:T(8,128)}, u32[]{:S(2)}) copy-start(f32[16,512]{1,0:T(8,128)} %fusion.147) | copy-start | bytes 98308
  538.3 8.6 %copy-start.40 = (f32[16,512]{1,0:T(8,128)S(1)}, f32[16,512]{1,0:T(8,128)}, u32[]{:S(2)}) copy-start(f32[16,512]{1,0:T(8,128)} %broadcast_divide_fusion.9) | copy-start | bytes 98308
  538.3 8.6 %copy-start.41 = (f32[16,512]{1,0:T(8,128)S(1)}, f32[16,512]{1,0:T(8,128)}, u32[]{:S(2)}) copy-start(f32[16,512]{1,0:T(8,128)} %broadcast_divide_fusion.7) | copy-start | bytes 98308
  538.3 8.6 %copy-start.42 = (f32[16,512]{1,0:T(8,128)S(1)}, f32[16,512]{1,0:T(8,128)}, u32[]{:S(2)}) copy-start(f32[16,512]{1,0:T(8,128)} %broadcast_divide_fusion.5) | copy-start | bytes 98308
  538.3 8.6 %copy-start.43 = (f32[16,512]{1,0:T(8,128)S(1)}, f32[16,512]{1,0:T(8,128)}, u32[]{:S(2)}) copy-start(f32[16,512]{1,0:T(8,128)} %broadcast_divide_fusion.3) | copy-start | bytes 98308
  538.3 8.6 %copy-start.51 = (f32[16,512]{1,0:T(8,128)S(1)}, f32[16,512]{1,0:T(8,128)}, u32[]{:S(2)}) copy-start(f32[16,512]{1,0:T(8,128)} %fusion.149) | copy-start | bytes 98308
  (4 other events, 3.9 us)
where the time goes:
time: 561 us; the launch traced here: 550 us
  other arithmetic  365 us (65%)
  local copies, waits for them, and re-layouts  98.5 us (18%)
  starting transfers between devices  38.9 us (7%)
  matrix products  23.3 us (4%)
  between operations  21.6 us (4%)
    div x11, other arithmetic, solve_layers(): factors.append(couple[layer_no + 1] / pivot)  145 us
    sub x10, other arithmetic, solve_layers(): pivot = pivot - couple[layer_no] * factors[-1]  144 us
    unnamed x131, local copies, waits for them, and re-layouts  38.3 us
    unnamed x12, other arithmetic  24.4 us
    ppermute x4, starting transfers between devices, extended(): lax.ppermute(lax.slice_in_dim(block, block.shape[dim] - width, None, axis...  17.3 us
    concatenate x2, other arithmetic, extended(): block = jnp.concatenate([low, block, high], axis=dim)  12.5 us
  transfers between devices with their start and end apart: 11, of which 1 were waited for; matrix products, arithmetic and copies ran while one was open for 64% of the time, Pallas kernels for 0%

commit v1 on v0

v1 whole, which is shorter than its diff:
```python
import functools
import math

import jax
import jax.numpy as jnp
import ml_dtypes
import numpy as np
from jax import lax
from jax.experimental import pallas as pl
from jax.experimental.pallas import tpu as pltpu
from jax.sharding import PartitionSpec as P

MESH = pl.DeviceIdType.MESH
F32 = jnp.float32
BF16 = jnp.bfloat16


def split_table(table):
    high = table.astype(np.float32).astype(ml_dtypes.bfloat16)
    low = (table - high.astype(np.float64)).astype(np.float32).astype(ml_dtypes.bfloat16)
    return high, low


@functools.lru_cache(maxsize=2)
def tables_y(count_x, count_y, total_y):
    block = total_y // (count_x * count_y)
    place = np.arange(total_y)
    angle = 2.0 * np.pi / total_y * (place[:, None] * place[None, :] % total_y)
    both = np.stack([np.cos(angle), -np.sin(angle)], axis=1) / math.sqrt(total_y)
    both = both.reshape(total_y, 2, count_x, count_y, block).transpose(2, 0, 3, 1, 4)
    return split_table(both.reshape(count_x, total_y, count_y * 2 * block))


@functools.lru_cache(maxsize=2)
def tables_x(total_x):
    place = np.arange(total_x)
    angle = 2.0 * np.pi / total_x * (place[:, None] * place[None, :] % total_x)
    scale = 1.0 / math.sqrt(total_x)
    return split_table(np.cos(angle) * scale) + split_table(np.sin(angle) * scale)


def pick(codes, table):
    return jnp.where(codes == 0, table[0], jnp.where(codes == 1, table[1], table[2]))


def dot3(a_high, a_low, b_high, b_low):
    dot = functools.partial(jnp.dot, preferred_element_type=F32)
    return dot(a_high, b_high) + (dot(a_high, b_low) + dot(a_low, b_high))


def step_kernel(
    nx, ny,
    buoy_t, lame_t, shear_t, piezo_t,
    stress_in, veloc_in, mat_in, thigh_in, tlow_in,
    stress_out, veloc_out, lines_out,
    s_ref, v_ref, m_ref, thigh, tlow,
    xs, xr, ys, yr, charge, cols, chigh, clow, sendbuf,
    in_sem, out_sem, hsend, hrecv, a_send, a_recv, b_send, b_recv,
):
    gx, gy = lax.axis_index("gx"), lax.axis_index("gy")
    me = gx * ny + gy
    total = nx * ny
    nz, cx, cy = m_ref.shape
    zc = nz // ny
    width = lines_out.shape[2] // zc

    loads = [
        pltpu.make_async_copy(src, dst, in_sem.at[no])
        for no, (src, dst) in enumerate(
            [(stress_in, s_ref), (veloc_in, v_ref), (mat_in, m_ref), (thigh_in, thigh), (tlow_in, tlow)]
        )
    ]
    for load in loads:
        load.start()

    barrier = pltpu.get_barrier_semaphore()

    def greet(step, carry):
        other = lax.rem(me + step, total)
        pl.semaphore_signal(
            barrier, inc=1, device_id=(other // ny, lax.rem(other, ny)), device_id_type=MESH
        )
        return carry

    lax.fori_loop(1, total, greet, 0)

    row = lax.broadcasted_iota(jnp.int32, (cx, cy), 0)
    lane = lax.broadcasted_iota(jnp.int32, (cx, cy), 1)

    def to_lane(value, source, target):
        return pltpu.roll(value, lax.rem(target - source + cy, cy), 1)

    has = (gx > 0, gx < nx - 1, gy > 0, gy < ny - 1)
    targets = ((gx - 1, gy), (gx + 1, gy), (gx, gy - 1), (gx, gy + 1))
    opposite = (1, 0, 3, 2)

    def halo_copy(turn, side):
        send, recv = (xs, xr) if side < 2 else (ys, yr)
        slot = turn * 2 + side % 2
        return pltpu.make_async_remote_copy(
            src_ref=send.at[slot],
            dst_ref=recv.at[slot],
            send_sem=hsend.at[turn * 4 + side],
            recv_sem=hrecv.at[turn * 4 + side],
            device_id=targets[side],
            device_id_type=MESH,
        )

    def halo_start(turn):
        for side in range(4):
            @pl.when(has[side])
            def _():
                halo_copy(turn, side).start()

    def halo_wait(turn):
        for side in range(4):
            @pl.when(has[side])
            def _():
                halo_copy(turn, side).wait_send()

            @pl.when(has[opposite[side]])
            def _():
                halo_copy(turn, side).wait_recv()

    for side in range(4):
        recv = xr if side < 2 else yr
        for turn in range(2):
            @pl.when(jnp.logical_not(has[opposite[side]]))
            def _():
                recv[turn * 2 + side % 2] = jnp.zeros(recv.shape[1:], F32)

    loads[0].wait()
    xs[0, 0] = s_ref[0, :, 0, :]
    xs[0, 1] = jnp.zeros((nz, cy), F32)
    xs[1, 0] = s_ref[3, :, cx - 1, :]
    xs[1, 1] = s_ref[4, :, cx - 1, :]

    def pack_stress(z, carry):
        low, high = carry
        low = jnp.where(lane == z, to_lane(s_ref[1, z], 0, z), low)
        high = jnp.where(lane == z, to_lane(s_ref[3, z], cy - 1, z), high)
        high = jnp.where(lane == nz + z, to_lane(s_ref[5, z], cy - 1, nz + z), high)
        return low, high

    empty = jnp.zeros((cx, cy), F32)
    low, high = lax.fori_loop(0, nz, pack_stress, (empty, empty))
    ys[0] = low
    ys[1] = high
    pl.semaphore_wait(barrier, total - 1)
    halo_start(0)
    loads[1].wait()
    loads[2].wait()
    halo_wait(0)

    def x_next(value, turn, item, z):
        edge = xr[turn * 2, item, pl.ds(z, 1), :]
        return jnp.where(row == cx - 1, edge, pltpu.roll(value, cx - 1, 0))

    def x_last(value, turn, item, z):
        edge = xr[turn * 2 + 1, item, pl.ds(z, 1), :]
        return jnp.where(row == 0, edge, pltpu.roll(value, 1, 0))

    def y_next(value, turn, item, z):
        edge = to_lane(yr[turn * 2], item * nz + z, cy - 1)
        return jnp.where(lane == cy - 1, edge, pltpu.roll(value, cy - 1, 1))

    def y_last(value, turn, item, z):
        edge = to_lane(yr[turn * 2 + 1], item * nz + z, 0)
        return jnp.where(lane == 0, edge, pltpu.roll(value, 1, 1))

    def above(ref, item, z):
        return jnp.where(z < nz - 1, ref[item, jnp.minimum(z + 1, nz - 1)], 0.0)

    def below(ref, item, z):
        return jnp.where(z > 0, ref[item, jnp.maximum(z - 1, 0)], 0.0)

    def move(z, carry):
        low, high = carry
        buoy = pick(m_ref[z], buoy_t)
        sxx, syy, szz, sxy, sxz, syz = (s_ref[item, z] for item in range(6))
        ux = v_ref[0, z] + buoy * (
            (x_next(sxx, 0, 0, z) - sxx) + (sxy - y_last(sxy, 0, 0, z)) + (sxz - below(s_ref, 4, z))
        )
        uy = v_ref[1, z] + buoy * (
            (sxy - x_last(sxy, 0, 0, z)) + (y_next(syy, 0, 0, z) - syy) + (syz - below(s_ref, 5, z))
        )
        uz = v_ref[2, z] + buoy * (
            (sxz - x_last(sxz, 0, 1, z)) + (syz - y_last(syz, 0, 1, z)) + (above(s_ref, 2, z) - szz)
        )
        v_ref[0, z] = ux
        v_ref[1, z] = uy
        v_ref[2, z] = uz
        low = jnp.where(lane == z, to_lane(ux, 0, z), low)
        low = jnp.where(lane == nz + z, to_lane(uz, 0, nz + z), low)
        high = jnp.where(lane == z, to_lane(uy, cy - 1, z), high)
        return low, high

    low, high = lax.fori_loop(0, nz, move, (empty, empty))
    xs[2, 0] = v_ref[1, :, 0, :]
    xs[2, 1] = v_ref[2, :, 0, :]
    xs[3, 0] = v_ref[0, :, cx - 1, :]
    xs[3, 1] = jnp.zeros((nz, cy), F32)
    ys[2] = low
    ys[3] = high
    halo_start(1)
    save_veloc = pltpu.make_async_copy(v_ref, veloc_out, out_sem.at[0])
    save_veloc.start()
    halo_wait(1)

    def strain(z, carry):
        mat = m_ref[z]
        lame, shear, piezo = pick(mat, lame_t), pick(mat, shear_t), pick(mat, piezo_t)
        ux, uy, uz = v_ref[0, z], v_ref[1, z], v_ref[2, z]
        strain_x = ux - x_last(ux, 1, 0, z)
        strain_y = uy - y_last(uy, 1, 0, z)
        strain_z = uz - below(v_ref, 2, z)
        spread = lame * (strain_x + strain_y + strain_z)
        twice = 2.0 * shear
        s_ref[0, z] = s_ref[0, z] + spread + twice * strain_x
        s_ref[1, z] = s_ref[1, z] + spread + twice * strain_y
        s_ref[2, z] = s_ref[2, z] + spread + twice * strain_z
        s_ref[3, z] = s_ref[3, z] + shear * (
            (y_next(ux, 1, 0, z) - ux) + (x_next(uy, 1, 0, z) - uy)
        )
        sxz = s_ref[4, z] + shear * ((above(v_ref, 0, z) - ux) + (x_next(uz, 1, 1, z) - uz))
        syz = s_ref[5, z] + shear * ((above(v_ref, 1, z) - uy) + (y_next(uz, 1, 1, z) - uz))
        s_ref[4, z] = sxz
        s_ref[5, z] = syz
        charge[z] = piezo * (sxz + syz)
        return carry

    def line_copy(other):
        return pltpu.make_async_remote_copy(
            src_ref=charge.at[pl.ds(other * zc, zc)],
            dst_ref=cols.at[gy],
            send_sem=a_send.at[other],
            recv_sem=a_recv.at[gy],
            device_id=(gx, other),
            device_id_type=MESH,
        )

    def arrived_line(other):
        return pltpu.make_async_remote_copy(
            src_ref=charge.at[pl.ds(other * zc, zc)],
            dst_ref=cols.at[other],
            send_sem=a_send.at[other],
            recv_sem=a_recv.at[other],
            device_id=(gx, other),
            device_id_type=MESH,
        )

    def chunk(step, carry):
        other = lax.rem(gy + step, ny)
        lax.fori_loop(other * zc, other * zc + zc, strain, 0)
        line_copy(other).start()
        return carry

    lax.fori_loop(1, ny, chunk, 0)
    lax.fori_loop(gy * zc, gy * zc + zc, strain, 0)
    save_stress = pltpu.make_async_copy(s_ref, stress_out, out_sem.at[1])
    save_stress.start()

    def store_cols(source, value):
        flat = value.reshape(zc * cx, cy)
        high = flat.astype(BF16)
        where = pl.ds(pl.multiple_of(source * cy, cy), cy)
        chigh[:, where] = high
        clow[:, where] = (flat - high.astype(F32)).astype(BF16)

    store_cols(gy, charge[pl.ds(gy * zc, zc)])

    def take_cols(step, carry):
        source = lax.rem(gy - step + ny, ny)
        arrived_line(source).wait_recv()
        store_cols(source, cols[source])
        return carry

    lax.fori_loop(1, ny, take_cols, 0)
    loads[3].wait()
    loads[4].wait()

    def block_copy(other):
        return pltpu.make_async_remote_copy(
            src_ref=sendbuf.at[other],
            dst_ref=lines_out.at[gy, pl.ds(pl.multiple_of(gx * cx, cx), cx), :],
            send_sem=b_send.at[other],
            recv_sem=b_recv.at[me],
            device_id=(other // ny, lax.rem(other, ny)),
            device_id_type=MESH,
        )

    def arrived_block(other):
        sx, sy = other // ny, lax.rem(other, ny)
        return pltpu.make_async_remote_copy(
            src_ref=sendbuf.at[other],
            dst_ref=lines_out.at[sy, pl.ds(pl.multiple_of(sx * cx, cx), cx), :],
            send_sem=b_send.at[other],
            recv_sem=b_recv.at[other],
            device_id=(sx, sy),
            device_id_type=MESH,
        )

    def transform(step, carry):
        target_x = lax.rem(gx + step, nx)
        value = dot3(chigh[...], clow[...], thigh[target_x], tlow[target_x])
        for target_y in range(ny):
            other = target_x * ny + target_y
            sendbuf[other] = jnp.concatenate(
                [
                    value[z * cx : (z + 1) * cx, target_y * width : (target_y + 1) * width]
                    for z in range(zc)
                ],
                axis=1,
            )
        for target_y in range(ny):
            other = target_x * ny + target_y

            @pl.when(other != me)
            def _():
                block_copy(other).start()

        return carry

    lax.fori_loop(1, nx + 1, transform, 0)
    own = pltpu.make_async_copy(
        sendbuf.at[me],
        lines_out.at[gy, pl.ds(pl.multiple_of(gx * cx, cx), cx), :],
        out_sem.at[2],
    )
    own.start()

    def finish_lines(step, carry):
        line_copy(lax.rem(gy + step, ny)).wait_send()
        return carry

    lax.fori_loop(1, ny, finish_lines, 0)

    def finish_blocks(step, carry):
        other = lax.rem(me + step, total)
        block_copy(other).wait_send()
        arrived_block(other).wait_recv()
        return carry

    lax.fori_loop(1, total, finish_blocks, 0)
    own.wait()
    save_veloc.wait()
    save_stress.wait()


def solve_kernel(
    ny, kinds, lateral_t, normal_t,
    lines, cos_high, cos_low, sin_high, sin_low, wave_x, wave_y,
    modes, high, low,
):
    me = lax.axis_index("gx") * ny + lax.axis_index("gy")
    width = lines.shape[2]
    _, nz, block, _ = modes.shape

    @pl.when(pl.program_id(0) == 0)
    def _():
        for source in range(ny):
            value = lines[source].T
            top = value.astype(BF16)
            high[source * width : (source + 1) * width, :] = top
            low[source * width : (source + 1) * width, :] = (value - top.astype(F32)).astype(BF16)

    with_cos = dot3(high[...], low[...], cos_high[...], cos_low[...])
    with_sin = dot3(high[...], low[...], sin_high[...], sin_low[...])

    def part(value, z, no):
        start = (z * 2 + no) * block
        return value[start : start + block]

    lateral = [pick(kinds[z], lateral_t) for z in range(nz)]
    normal = [pick(kinds[z], normal_t) for z in range(nz)]
    couple = [normal[0]] + [0.5 * (normal[z - 1] + normal[z]) for z in range(1, nz)] + [normal[-1]]
    wave = wave_y[me][:, :1] + wave_x[...]
    factors, reals, imags = [], [], []
    for z in range(nz):
        real = part(with_cos, z, 0) + part(with_sin, z, 1)
        imag = part(with_cos, z, 1) - part(with_sin, z, 0)
        pivot = couple[z] + couple[z + 1] + wave * lateral[z]
        if z > 0:
            pivot = pivot - couple[z] * factors[-1]
            real = real + couple[z] * reals[-1]
            imag = imag + couple[z] * imags[-1]
        inverse = 1.0 / pivot
        factors.append(couple[z + 1] * inverse)
        reals.append(real * inverse)
        imags.append(imag * inverse)
    real, imag = reals[-1], imags[-1]
    for z in range(nz - 1, -1, -1):
        if z < nz - 1:
            real = reals[z] + factors[z] * real
            imag = imags[z] + factors[z] * imag
        modes[0, z] = real
        modes[1, z] = imag


def per_device(
    nx, ny, stress, velocity, material, layer_kind,
    buoyancy, lame_first, shear_modulus, piezo, permit_lateral, permit_normal,
):
    nz, cx, cy = material.shape
    total_x, total_y = cx * nx, cy * ny
    total = nx * ny
    block = total_y // total
    zc = nz // ny
    width = zc * 2 * block
    smem = pl.BlockSpec(memory_space=pltpu.SMEM)
    hbm = pl.BlockSpec(memory_space=pl.ANY)
    thigh, tlow = tables_y(nx, ny, total_y)
    stress_next, velocity_next, lines = pl.pallas_call(
        functools.partial(step_kernel, nx, ny),
        out_shape=(
            jax.ShapeDtypeStruct(stress.shape, F32),
            jax.ShapeDtypeStruct(velocity.shape, F32),
            jax.ShapeDtypeStruct((ny, total_x, width), F32),
        ),
        in_specs=[smem] * 4 + [hbm] * 5,
        out_specs=(hbm, hbm, hbm),
        scratch_shapes=[
            pltpu.VMEM(stress.shape, F32),
            pltpu.VMEM(velocity.shape, F32),
            pltpu.VMEM(material.shape, jnp.int32),
            pltpu.VMEM(thigh.shape, BF16),
            pltpu.VMEM(tlow.shape, BF16),
            pltpu.VMEM((4, 2, nz, cy), F32),
            pltpu.VMEM((4, 2, nz, cy), F32),
            pltpu.VMEM((4, cx, cy), F32),
            pltpu.VMEM((4, cx, cy), F32),
            pltpu.VMEM((nz, cx, cy), F32),
            pltpu.VMEM((ny, zc, cx, cy), F32),
            pltpu.VMEM((zc * cx, total_y), BF16),
            pltpu.VMEM((zc * cx, total_y), BF16),
            pltpu.VMEM((total, cx, width), F32),
            pltpu.SemaphoreType.DMA((5,)),
            pltpu.SemaphoreType.DMA((3,)),
            pltpu.SemaphoreType.DMA((8,)),
            pltpu.SemaphoreType.DMA((8,)),
            pltpu.SemaphoreType.DMA((ny,)),
            pltpu.SemaphoreType.DMA((ny,)),
            pltpu.SemaphoreType.DMA((total,)),
            pltpu.SemaphoreType.DMA((total,)),
        ],
        compiler_params=pltpu.CompilerParams(
            collective_id=0, has_side_effects=True, vmem_limit_bytes=56 * 2**20
        ),
        name="elastic_and_lines",
    )(
        buoyancy, lame_first, shear_modulus, piezo,
        stress, velocity, material, jnp.asarray(thigh), jnp.asarray(tlow),
    )

    columns = min(256, total_x)
    wave_x = (2.0 * np.sin(np.pi * np.arange(total_x) / total_x)) ** 2
    wave_y = (2.0 * np.sin(np.pi * np.arange(total_y) / total_y)) ** 2
    wave_y = np.broadcast_to(wave_y.reshape(total, block, 1), (total, block, 128))
    table_spec = pl.BlockSpec((total_x, columns), lambda i: (0, i))
    modes = pl.pallas_call(
        functools.partial(solve_kernel, ny),
        grid=(total_x // columns,),
        out_shape=jax.ShapeDtypeStruct((2, nz, block, total_x), F32),
        in_specs=[smem] * 3
        + [pl.BlockSpec((ny, total_x, width), lambda i: (0, 0, 0))]
        + [table_spec] * 4
        + [
            pl.BlockSpec((1, columns), lambda i: (0, i)),
            pl.BlockSpec((total, block, 128), lambda i: (0, 0, 0)),
        ],
        out_specs=pl.BlockSpec((2, nz, block, columns), lambda i: (0, 0, 0, i)),
        scratch_shapes=[
            pltpu.VMEM((ny * width, total_x), BF16),
            pltpu.VMEM((ny * width, total_x), BF16),
        ],
        compiler_params=pltpu.CompilerParams(vmem_limit_bytes=56 * 2**20),
        name="lines_and_solve",
    )(
        layer_kind, permit_lateral, permit_normal, lines,
        *[jnp.asarray(table) for table in tables_x(total_x)],
        jnp.asarray(wave_x.reshape(1, -1), F32), jnp.asarray(wave_y, F32),
    )
    return stress_next, velocity_next, modes


def solution(mesh):
    cells = P(None, None, "gx", "gy")
    in_specs = (cells, cells, P(None, "gx", "gy")) + (P(),) * 7
    out_specs = (cells, cells, P(None, None, ("gx", "gy"), None))
    return jax.shard_map(
        functools.partial(per_device, mesh.shape["gx"], mesh.shape["gy"]),
        mesh=mesh, in_specs=in_specs, out_specs=out_specs, check_vma=False,
    )
```

time: 561 us -> 64 us (0.11); the launches traced: 550 us -> 63.8 us
  other arithmetic: 365 us -> 0 us
  local copies, waits for them, and re-layouts: 98.5 us -> 3.66 us
  Pallas kernels: 0 us -> 59.5 us
  starting transfers between devices: 38.9 us -> 0 us
  matrix products: 23.3 us -> 0 us
  between operations: 21.6 us -> 0.66 us
    div x12 -> x0, other arithmetic: 153 us -> none  [the longest x11 145 us: solve_layers(): factors.append(couple[layer_no + 1] / pivot)]
    sub x10 -> x0, other arithmetic: 144 us -> none  [solve_layers(): pivot = pivot - couple[layer_no] * factors[-1]]
    pallas_call x0 -> x2, Pallas kernels: none -> 59.5 us  [the longest x1 54.3 us: per_device(): pl.pallas_call(functools.partial(step_kernel, nx, ny), out_shape=(jax.Sha...]
    unnamed x131 -> x6, local copies, waits for them, and re-layouts: 38.3 us -> 3.66 us
    unnamed x12 -> x0, other arithmetic: 24.4 us -> none
    dot_general x4 -> x0, matrix products: 23.3 us -> none  [the longest x1 6.41 us: per_device(): jnp.einsum('zxy,yk->zxk', columns, sin_y, precision=lax.Precision.HIGHEST)]
    ppermute x8 -> x0, starting transfers between devices: 22.6 us -> none  [the longest x4 17.3 us: extended(): lax.ppermute(lax.slice_in_dim(block, block.shape[dim] - width, None, axis...]
    slice x19 -> x0, local copies, waits for them, and re-layouts: 19 us -> none  [the longest x6 5.33 us: lookup(): result = result + jnp.where(codes == material_no, table[material_no], 0.0)]
  transfers between devices with their start and end apart: 11 -> 0, of which waited for: 1 -> 0; matrix products, arithmetic and copies ran while one was open for 64% -> 0% of each run, Pallas kernels for 0% -> 0%
where the time goes in v1:
time: 64 us; the launch traced here: 63.8 us
  Pallas kernels  59.5 us (93%)
  local copies, waits for them, and re-layouts  3.66 us (6%)
  between operations  0.66 us (1%)
    pallas_call x1, Pallas kernels, per_device(): pl.pallas_call(functools.partial(step_kernel, nx, ny), out_shape=(jax.Sha...  54.3 us
    pallas_call x1, Pallas kernels, per_device(): pl.pallas_call(functools.partial(solve_kernel, ny), grid=(total_x // colu...  5.19 us
    unnamed x6, local copies, waits for them, and re-layouts  3.66 us

profile of v1, /device:TPU:0, one launch (start us, length us, event | category | flops | bytes accessed | tf_op | source)
XLA Modules:
  0.0 63.8 jit_solution(8657751412697362696)
XLA Ops:
  0.6 54.3 %elastic_and_lines.1 = (f32[6,16,64,128]{3,2,1,0:T(8,128)}, f32[3,16,64,128]{3,2,1,0:T(8,128)}, f32[4,512,128]{2,1,0:T(8,128)}) custom-call(f32[3]{0:T(128)} %buoy_t.1, f32[3]{0:T(128)} %lame_t.1, f32[3]{0:T(128)} %shear_t.1, f32[3]{0:T(128)} %piezo_t.1, f32[6,16,64,128]{3,2,1,0:T(8,128)} %stress_in.1, f32[3,16,64,128]{3,2,1,0:T(8,128)} %veloc_in.1, ...), custom_call_target="tpu_custom_call" | custom-call | tf_op jit(solution)/shard_map/elastic_and_lines/pallas_call | solution.py:413
  55.0 0.0 copy-start
  55.0 5.2 %lines_and_solve.1 = f32[2,16,16,512]{3,2,1,0:T(8,128)} custom-call(s32[16]{0:T(128)} %kinds.1, f32[3]{0:T(128)} %lateral_t.1, f32[3]{0:T(128)} %normal_t.1, f32[4,512,128]{2,1,0:T(8,128)} %get-tuple-element.8.lines, bf16[512,512]{1,0:T(8,128)(2,1)} %constant.18.clone.cos_high, bf16[512,512]{1,0:T(8,128)(2,1)} %constant.19.clone.cos_low, ...), custom_call_target="tpu_custom_call" | custom-call | tf_op jit(solution)/shard_map/lines_and_solve/pallas_call | solution.py:460
  60.2 0.0 copy-done
  60.2 0.0 copy-start.1
  60.2 1.7 %copy.23 = f32[6,16,64,128]{3,2,1,0:T(8,128)} copy(f32[6,16,64,128]{3,2,1,0:T(8,128)S(1)} %copy-done) | data formatting | bytes 6291456
  61.8 0.8 %copy-done.1 = f32[3,16,64,128]{3,2,1,0:T(8,128)S(1)} copy-done((f32[3,16,64,128]{3,2,1,0:T(8,128)S(1)}, f32[3,16,64,128]{3,2,1,0:T(8,128)}, u32[]{:S(2)}) %copy-start.1) | copy-done | bytes 1572888
  62.7 1.1 %copy.24 = f32[3,16,64,128]{3,2,1,0:T(8,128)} copy(f32[3,16,64,128]{3,2,1,0:T(8,128)S(1)} %copy-done.1) | data formatting | bytes 3145728
Async XLA Ops:
  55.0 5.2 %copy-start = (f32[6,16,64,128]{3,2,1,0:T(8,128)S(1)}, f32[6,16,64,128]{3,2,1,0:T(8,128)}, u32[]{:S(2)}) copy-start(f32[6,16,64,128]{3,2,1,0:T(8,128)} %get-tuple-element.12) | copy-start | bytes 9437188
  60.2 2.5 %copy-start.1 = (f32[3,16,64,128]{3,2,1,0:T(8,128)S(1)}, f32[3,16,64,128]{3,2,1,0:T(8,128)}, u32[]{:S(2)}) copy-start(f32[3,16,64,128]{3,2,1,0:T(8,128)} %get-tuple-element.13) | copy-start | bytes 4718596

commit v2 on v1

--- a/solution.py
+++ b/solution.py
@@ -24,11 +24,12 @@
 @functools.lru_cache(maxsize=2)
 def tables_y(count_x, count_y, total_y):
     block = total_y // (count_x * count_y)
+    half = count_y // 2
     place = np.arange(total_y)
     angle = 2.0 * np.pi / total_y * (place[:, None] * place[None, :] % total_y)
     both = np.stack([np.cos(angle), -np.sin(angle)], axis=1) / math.sqrt(total_y)
-    both = both.reshape(total_y, 2, count_x, count_y, block).transpose(2, 0, 3, 1, 4)
-    return split_table(both.reshape(count_x, total_y, count_y * 2 * block))
+    both = both.reshape(total_y, 2, count_x // 2, 2, 2, half, block).transpose(4, 2, 0, 3, 5, 1, 6)
+    return split_table(both.reshape(2, count_x // 2, total_y, 4 * half * block))
 
 
 @functools.lru_cache(maxsize=2)
@@ -55,19 +56,25 @@
     stress_out, veloc_out, lines_out,
     s_ref, v_ref, m_ref, thigh, tlow,
     xs, xr, ys, yr, charge, cols, chigh, clow, sendbuf,
-    in_sem, out_sem, hsend, hrecv, a_send, a_recv, b_send, b_recv,
+    in_sem, out_sem, own_sem, hsend, hrecv, a_send, a_recv, b_send, b_recv,
 ):
     gx, gy = lax.axis_index("gx"), lax.axis_index("gy")
     me = gx * ny + gy
     total = nx * ny
     nz, cx, cy = m_ref.shape
-    zc = nz // ny
+    chunks = lines_out.shape[0]
+    zc = nz // chunks
     width = lines_out.shape[2] // zc
+    half = ny // 2
+    side_y = gy // half
+    hubs = (half - 1, half)
+    is_hub = jnp.logical_or(gy == hubs[0], gy == hubs[1])
+    my_hub = half - 1 + side_y
 
     loads = [
         pltpu.make_async_copy(src, dst, in_sem.at[no])
         for no, (src, dst) in enumerate(
-            [(stress_in, s_ref), (veloc_in, v_ref), (mat_in, m_ref), (thigh_in, thigh), (tlow_in, tlow)]
+            [(stress_in, s_ref), (veloc_in, v_ref), (mat_in, m_ref), (thigh_in.at[side_y], thigh), (tlow_in.at[side_y], tlow)]
         )
     ]
     for load in loads:
@@ -229,34 +236,36 @@
         charge[z] = piezo * (sxz + syz)
         return carry
 
-    def line_copy(other):
+    def raw_copy(no, which):
         return pltpu.make_async_remote_copy(
-            src_ref=charge.at[pl.ds(other * zc, zc)],
-            dst_ref=cols.at[gy],
-            send_sem=a_send.at[other],
-            recv_sem=a_recv.at[gy],
-            device_id=(gx, other),
+            src_ref=charge.at[pl.ds(no * zc, zc)],
+            dst_ref=cols.at[no, gy],
+            send_sem=a_send.at[no, which],
+            recv_sem=a_recv.at[no, gy],
+            device_id=(gx, hubs[which]),
             device_id_type=MESH,
         )
 
-    def arrived_line(other):
+    def arrived_raw(no, source):
         return pltpu.make_async_remote_copy(
-            src_ref=charge.at[pl.ds(other * zc, zc)],
-            dst_ref=cols.at[other],
-            send_sem=a_send.at[other],
-            recv_sem=a_recv.at[other],
-            device_id=(gx, other),
+            src_ref=charge.at[pl.ds(no * zc, zc)],
+            dst_ref=cols.at[no, source],
+            send_sem=a_send.at[no, 0],
+            recv_sem=a_recv.at[no, source],
+            device_id=(gx, source),
             device_id_type=MESH,
         )
 
-    def chunk(step, carry):
-        other = lax.rem(gy + step, ny)
-        lax.fori_loop(other * zc, other * zc + zc, strain, 0)
-        line_copy(other).start()
+    def chunk(no, carry):
+        lax.fori_loop(no * zc, no * zc + zc, strain, 0)
+        for which in range(2):
+            @pl.when(gy != hubs[which])
+            def _():
+                raw_copy(no, which).start()
+
         return carry
 
-    lax.fori_loop(1, ny, chunk, 0)
-    lax.fori_loop(gy * zc, gy * zc + zc, strain, 0)
+    lax.fori_loop(0, chunks, chunk, 0)
     save_stress = pltpu.make_async_copy(s_ref, stress_out, out_sem.at[1])
     save_stress.start()
 
@@ -267,98 +276,133 @@
         chigh[:, where] = high
         clow[:, where] = (flat - high.astype(F32)).astype(BF16)
 
-    store_cols(gy, charge[pl.ds(gy * zc, zc)])
-
-    def take_cols(step, carry):
-        source = lax.rem(gy - step + ny, ny)
-        arrived_line(source).wait_recv()
-        store_cols(source, cols[source])
-        return carry
-
-    lax.fori_loop(1, ny, take_cols, 0)
     loads[3].wait()
     loads[4].wait()
-
-    def block_copy(other):
+    my_rows = pl.ds(pl.multiple_of(gx * cx, cx), cx)
+
+    def block_copy(no, tx, ty):
         return pltpu.make_async_remote_copy(
-            src_ref=sendbuf.at[other],
-            dst_ref=lines_out.at[gy, pl.ds(pl.multiple_of(gx * cx, cx), cx), :],
-            send_sem=b_send.at[other],
-            recv_sem=b_recv.at[me],
-            device_id=(other // ny, lax.rem(other, ny)),
+            src_ref=sendbuf.at[no, tx * half + ty],
+            dst_ref=lines_out.at[no, my_rows, :],
+            send_sem=b_send.at[no, tx * half + ty],
+            recv_sem=b_recv.at[no, gx],
+            device_id=(tx, side_y * half + ty),
             device_id_type=MESH,
         )
 
-    def arrived_block(other):
-        sx, sy = other // ny, lax.rem(other, ny)
+    def own_copy(no):
+        return pltpu.make_async_copy(
+            sendbuf.at[no, gx * half + lax.rem(gy, half)],
+            lines_out.at[no, my_rows, :],
+            own_sem.at[no],
+        )
+
+    def arrived_block(no, source):
         return pltpu.make_async_remote_copy(
-            src_ref=sendbuf.at[other],
-            dst_ref=lines_out.at[sy, pl.ds(pl.multiple_of(sx * cx, cx), cx), :],
-            send_sem=b_send.at[other],
-            recv_sem=b_recv.at[other],
-            device_id=(sx, sy),
+            src_ref=sendbuf.at[no, 0],
+            dst_ref=lines_out.at[no, pl.ds(pl.multiple_of(source * cx, cx), cx), :],
+            send_sem=b_send.at[no, 0],
+            recv_sem=b_recv.at[no, source],
+            device_id=(source, my_hub),
             device_id_type=MESH,
         )
 
-    def transform(step, carry):
-        target_x = lax.rem(gx + step, nx)
-        value = dot3(chigh[...], clow[...], thigh[target_x], tlow[target_x])
-        for target_y in range(ny):
-            other = target_x * ny + target_y
-            sendbuf[other] = jnp.concatenate(
-                [
-                    value[z * cx : (z + 1) * cx, target_y * width : (target_y + 1) * width]
-                    for z in range(zc)
-                ],
-                axis=1,
-            )
-        for target_y in range(ny):
-            other = target_x * ny + target_y
-
-            @pl.when(other != me)
-            def _():
-                block_copy(other).start()
-
-        return carry
-
-    lax.fori_loop(1, nx + 1, transform, 0)
-    own = pltpu.make_async_copy(
-        sendbuf.at[me],
-        lines_out.at[gy, pl.ds(pl.multiple_of(gx * cx, cx), cx), :],
-        out_sem.at[2],
-    )
-    own.start()
-
-    def finish_lines(step, carry):
-        line_copy(lax.rem(gy + step, ny)).wait_send()
-        return carry
-
-    lax.fori_loop(1, ny, finish_lines, 0)
-
-    def finish_blocks(step, carry):
-        other = lax.rem(me + step, total)
-        block_copy(other).wait_send()
-        arrived_block(other).wait_recv()
-        return carry
-
-    lax.fori_loop(1, total, finish_blocks, 0)
-    own.wait()
+    def is_me(tx, ty):
+        return jnp.logical_and(tx == gx, side_y * half + ty == gy)
+
+    @pl.when(is_hub)
+    def _():
+        def hub_chunk(no, carry):
+            store_cols(gy, charge[pl.ds(no * zc, zc)])
+
+            def take(step, carry):
+                source = lax.rem(gy + step, ny)
+                arrived_raw(no, source).wait_recv()
+                store_cols(source, cols[no, source])
+                return carry
+
+            lax.fori_loop(1, ny, take, 0)
+
+            def transform(step, carry):
+                pair = lax.rem(gx // 2 + step, nx // 2)
+                value = dot3(chigh[...], clow[...], thigh[pair], tlow[pair])
+                for i in range(2):
+                    for ty in range(half):
+                        tx = pair * 2 + i
+                        first = (i * half + ty) * width
+                        sendbuf[no, tx * half + ty] = jnp.concatenate(
+                            [
+                                value[z * cx : (z + 1) * cx, first : first + width]
+                                for z in range(zc)
+                            ],
+                            axis=1,
+                        )
+
+                        @pl.when(jnp.logical_not(is_me(tx, ty)))
+                        def _():
+                            block_copy(no, tx, ty).start()
+
+                return carry
+
+            lax.fori_loop(1, nx // 2 + 1, transform, 0)
+            own_copy(no).start()
+            return carry
+
+        lax.fori_loop(0, chunks, hub_chunk, 0)
+
+        def finish_sends(no, carry):
+            own_copy(no).wait()
+
+            def finish_target(tx, carry):
+                for ty in range(half):
+                    @pl.when(jnp.logical_not(is_me(tx, ty)))
+                    def _():
+                        block_copy(no, tx, ty).wait_send()
+
+                return carry
+
+            return lax.fori_loop(0, nx, finish_target, carry)
+
+        lax.fori_loop(0, chunks, finish_sends, 0)
+
+    def finish(no, carry):
+        for which in range(2):
+            @pl.when(gy != hubs[which])
+            def _():
+                raw_copy(no, which).wait_send()
+
+        def finish_source(source, carry):
+            @pl.when(jnp.logical_not(jnp.logical_and(source == gx, is_hub)))
+            def _():
+                arrived_block(no, source).wait_recv()
+
+            return carry
+
+        return lax.fori_loop(0, nx, finish_source, carry)
+
+    lax.fori_loop(0, chunks, finish, 0)
     save_veloc.wait()
     save_stress.wait()
 
 
 def solve_kernel(
     ny, kinds, lateral_t, normal_t,
-    lines, cos_high, cos_low, sin_high, sin_low, wave_x, wave_y,
-    modes, high, low,
+    lines, cos_high, cos_low, sin_high, sin_low, wave_x, wave_y, stress, veloc,
+    modes, stress_out, veloc_out, high, low, sem,
 ):
     me = lax.axis_index("gx") * ny + lax.axis_index("gy")
     width = lines.shape[2]
     _, nz, block, _ = modes.shape
+    copies = [
+        pltpu.make_async_copy(stress, stress_out, sem.at[0]),
+        pltpu.make_async_copy(veloc, veloc_out, sem.at[1]),
+    ]
 
     @pl.when(pl.program_id(0) == 0)
     def _():
-        for source in range(ny):
+        for copy in copies:
+            copy.start()
+        for source in range(lines.shape[0]):
             value = lines[source].T
             top = value.astype(BF16)
             high[source * width : (source + 1) * width, :] = top
@@ -396,6 +440,11 @@
         modes[0, z] = real
         modes[1, z] = imag
 
+    @pl.when(pl.program_id(0) == pl.num_programs(0) - 1)
+    def _():
+        for copy in copies:
+            copy.wait()
+
 
 def per_device(
     nx, ny, stress, velocity, material, layer_kind,
@@ -405,7 +454,8 @@
     total_x, total_y = cx * nx, cy * ny
     total = nx * ny
     block = total_y // total
-    zc = nz // ny
+    zc = max(1, min(nz, 128 // (2 * block)))
+    chunks = nz // zc
     width = zc * 2 * block
     smem = pl.BlockSpec(memory_space=pltpu.SMEM)
     hbm = pl.BlockSpec(memory_space=pl.ANY)
@@ -415,7 +465,7 @@
         out_shape=(
             jax.ShapeDtypeStruct(stress.shape, F32),
             jax.ShapeDtypeStruct(velocity.shape, F32),
-            jax.ShapeDtypeStruct((ny, total_x, width), F32),
+            jax.ShapeDtypeStruct((chunks, total_x, width), F32),
         ),
         in_specs=[smem] * 4 + [hbm] * 5,
         out_specs=(hbm, hbm, hbm),
@@ -423,25 +473,26 @@
             pltpu.VMEM(stress.shape, F32),
             pltpu.VMEM(velocity.shape, F32),
             pltpu.VMEM(material.shape, jnp.int32),
-            pltpu.VMEM(thigh.shape, BF16),
-            pltpu.VMEM(tlow.shape, BF16),
+            pltpu.VMEM(thigh.shape[1:], BF16),
+            pltpu.VMEM(tlow.shape[1:], BF16),
             pltpu.VMEM((4, 2, nz, cy), F32),
             pltpu.VMEM((4, 2, nz, cy), F32),
             pltpu.VMEM((4, cx, cy), F32),
             pltpu.VMEM((4, cx, cy), F32),
             pltpu.VMEM((nz, cx, cy), F32),
-            pltpu.VMEM((ny, zc, cx, cy), F32),
+            pltpu.VMEM((chunks, ny, zc, cx, cy), F32),
             pltpu.VMEM((zc * cx, total_y), BF16),
             pltpu.VMEM((zc * cx, total_y), BF16),
-            pltpu.VMEM((total, cx, width), F32),
+            pltpu.VMEM((chunks, total // 2, cx, width), F32),
             pltpu.SemaphoreType.DMA((5,)),
-            pltpu.SemaphoreType.DMA((3,)),
+            pltpu.SemaphoreType.DMA((2,)),
+            pltpu.SemaphoreType.DMA((chunks,)),
             pltpu.SemaphoreType.DMA((8,)),
             pltpu.SemaphoreType.DMA((8,)),
-            pltpu.SemaphoreType.DMA((ny,)),
-            pltpu.SemaphoreType.DMA((ny,)),
-            pltpu.SemaphoreType.DMA((total,)),
-            pltpu.SemaphoreType.DMA((total,)),
+            pltpu.SemaphoreType.DMA((chunks, 2)),
+            pltpu.SemaphoreType.DMA((chunks, ny)),
+            pltpu.SemaphoreType.DMA((chunks, total // 2)),
+            pltpu.SemaphoreType.DMA((chunks, nx)),
         ],
         compiler_params=pltpu.CompilerParams(
             collective_id=0, has_side_effects=True, vmem_limit_bytes=56 * 2**20
@@ -457,21 +508,28 @@
     wave_y = (2.0 * np.sin(np.pi * np.arange(total_y) / total_y)) ** 2
     wave_y = np.broadcast_to(wave_y.reshape(total, block, 1), (total, block, 128))
     table_spec = pl.BlockSpec((total_x, columns), lambda i: (0, i))
-    modes = pl.pallas_call(
+    modes, stress_next, velocity_next = pl.pallas_call(
         functools.partial(solve_kernel, ny),
         grid=(total_x // columns,),
-        out_shape=jax.ShapeDtypeStruct((2, nz, block, total_x), F32),
+        out_shape=(
+            jax.ShapeDtypeStruct((2, nz, block, total_x), F32),
+            jax.ShapeDtypeStruct(stress.shape, F32),
+            jax.ShapeDtypeStruct(velocity.shape, F32),
+        ),
         in_specs=[smem] * 3
-        + [pl.BlockSpec((ny, total_x, width), lambda i: (0, 0, 0))]
+        + [pl.BlockSpec((chunks, total_x, width), lambda i: (0, 0, 0))]
         + [table_spec] * 4
         + [
             pl.BlockSpec((1, columns), lambda i: (0, i)),
             pl.BlockSpec((total, block, 128), lambda i: (0, 0, 0)),
+            hbm,
+            hbm,
         ],
-        out_specs=pl.BlockSpec((2, nz, block, columns), lambda i: (0, 0, 0, i)),
+        out_specs=(pl.BlockSpec((2, nz, block, columns), lambda i: (0, 0, 0, i)), hbm, hbm),
         scratch_shapes=[
-            pltpu.VMEM((ny * width, total_x), BF16),
-            pltpu.VMEM((ny * width, total_x), BF16),
+            pltpu.VMEM((chunks * width, total_x), BF16),
+            pltpu.VMEM((chunks * width, total_x), BF16),
+            pltpu.SemaphoreType.DMA((2,)),
         ],
         compiler_params=pltpu.CompilerParams(vmem_limit_bytes=56 * 2**20),
         name="lines_and_solve",
@@ -479,6 +537,7 @@
         layer_kind, permit_lateral, permit_normal, lines,
         *[jnp.asarray(table) for table in tables_x(total_x)],
         jnp.asarray(wave_x.reshape(1, -1), F32), jnp.asarray(wave_y, F32),
+        stress_next, velocity_next,
     )
     return stress_next, velocity_next, modes
 

time: 64 us -> 199 us (3.11)
  Pallas kernels: 59.5 us -> 198 us
  local copies, waits for them, and re-layouts: 3.66 us -> 0 us
    pallas_call x1, Pallas kernels: 5.19 us -> 147 us  [per_device(): pl.pallas_call(functools.partial(solve_kernel, ny), grid=(total_x // colu...]
    unnamed x6 -> x0, local copies, waits for them, and re-layouts: 3.66 us -> none
    pallas_call x1, Pallas kernels: 54.3 us -> 51.2 us  [per_device(): pl.pallas_call(functools.partial(step_kernel, nx, ny), out_shape=(jax.Sha...]
where the time goes in v2:
time: 199 us
  Pallas kernels  198 us (99%)
    pallas_call x1, Pallas kernels, per_device(): pl.pallas_call(functools.partial(solve_kernel, ny), grid=(total_x // colu...  147 us
    pallas_call x1, Pallas kernels, per_device(): pl.pallas_call(functools.partial(step_kernel, nx, ny), out_shape=(jax.Sha...  51.2 us

profile of v2, /device:TPU:0, one launch (start us, length us, event | category | flops | bytes accessed | tf_op | source)
XLA Modules:
  0.0 198.5 jit_solution(4540033518290107018)
XLA Ops:
  0.6 51.2 %elastic_and_lines.1 = (f32[6,16,64,128]{3,2,1,0:T(8,128)}, f32[3,16,64,128]{3,2,1,0:T(8,128)}, f32[4,512,128]{2,1,0:T(8,128)}) custom-call(f32[3]{0:T(128)} %buoy_t.1, f32[3]{0:T(128)} %lame_t.1, f32[3]{0:T(128)} %shear_t.1, f32[3]{0:T(128)} %piezo_t.1, f32[6,16,64,128]{3,2,1,0:T(8,128)} %stress_in.1, f32[3,16,64,128]{3,2,1,0:T(8,128)} %veloc_in.1, ...), custom_call_target="tpu_custom_call" | custom-call | tf_op jit(solution)/shard_map/elastic_and_lines/pallas_call | solution.py:463
  51.8 146.7 %lines_and_solve.1 = (f32[2,16,16,512]{3,2,1,0:T(8,128)}, f32[6,16,64,128]{3,2,1,0:T(8,128)}, f32[3,16,64,128]{3,2,1,0:T(8,128)}) custom-call(s32[16]{0:T(128)} %kinds.1, f32[3]{0:T(128)} %lateral_t.1, f32[3]{0:T(128)} %normal_t.1, f32[4,512,128]{2,1,0:T(8,128)} %get-tuple-element.9.lines, bf16[512,512]{1,0:T(8,128)(2,1)} %constant.18.clone.cos_high, ...), custom_call_target="tpu_custom_call" | custom-call | tf_op jit(solution)/shard_map/lines_and_solve/pallas_call | solution.py:511

commit v3 on v2

--- a/solution.py
+++ b/solution.py
@@ -113,14 +113,17 @@
             device_id_type=MESH,
         )
 
+    def sides(turn):
+        return (0, 2) if turn == 1 else range(4)
+
     def halo_start(turn):
-        for side in range(4):
+        for side in sides(turn):
             @pl.when(has[side])
             def _():
                 halo_copy(turn, side).start()
 
     def halo_wait(turn):
-        for side in range(4):
+        for side in sides(turn):
             @pl.when(has[side])
             def _():
                 halo_copy(turn, side).wait_send()
@@ -131,7 +134,7 @@
 
     for side in range(4):
         recv = xr if side < 2 else yr
-        for turn in range(2):
+        for turn in range(3):
             @pl.when(jnp.logical_not(has[opposite[side]]))
             def _():
                 recv[turn * 2 + side % 2] = jnp.zeros(recv.shape[1:], F32)
@@ -181,59 +184,72 @@
     def below(ref, item, z):
         return jnp.where(z > 0, ref[item, jnp.maximum(z - 1, 0)], 0.0)
 
-    def move(z, carry):
+    def move_z(z, low):
+        sxz, syz, szz = s_ref[4, z], s_ref[5, z], s_ref[2, z]
+        uz = v_ref[2, z] + pick(m_ref[z], buoy_t) * (
+            (sxz - x_last(sxz, 0, 1, z)) + (syz - y_last(syz, 0, 1, z)) + (above(s_ref, 2, z) - szz)
+        )
+        v_ref[2, z] = uz
+        return jnp.where(lane == z, to_lane(uz, 0, z), low)
+
+    low = lax.fori_loop(0, nz, move_z, empty)
+    xs[2, 0] = v_ref[2, :, 0, :]
+    xs[2, 1] = jnp.zeros((nz, cy), F32)
+    ys[2] = low
+    halo_start(1)
+
+    def move_xy(z, carry):
         low, high = carry
         buoy = pick(m_ref[z], buoy_t)
-        sxx, syy, szz, sxy, sxz, syz = (s_ref[item, z] for item in range(6))
+        sxx, syy, sxy, sxz, syz = (s_ref[item, z] for item in (0, 1, 3, 4, 5))
         ux = v_ref[0, z] + buoy * (
             (x_next(sxx, 0, 0, z) - sxx) + (sxy - y_last(sxy, 0, 0, z)) + (sxz - below(s_ref, 4, z))
         )
         uy = v_ref[1, z] + buoy * (
             (sxy - x_last(sxy, 0, 0, z)) + (y_next(syy, 0, 0, z) - syy) + (syz - below(s_ref, 5, z))
         )
-        uz = v_ref[2, z] + buoy * (
-            (sxz - x_last(sxz, 0, 1, z)) + (syz - y_last(syz, 0, 1, z)) + (above(s_ref, 2, z) - szz)
-        )
         v_ref[0, z] = ux
         v_ref[1, z] = uy
-        v_ref[2, z] = uz
         low = jnp.where(lane == z, to_lane(ux, 0, z), low)
-        low = jnp.where(lane == nz + z, to_lane(uz, 0, nz + z), low)
         high = jnp.where(lane == z, to_lane(uy, cy - 1, z), high)
         return low, high
 
-    low, high = lax.fori_loop(0, nz, move, (empty, empty))
-    xs[2, 0] = v_ref[1, :, 0, :]
-    xs[2, 1] = v_ref[2, :, 0, :]
-    xs[3, 0] = v_ref[0, :, cx - 1, :]
-    xs[3, 1] = jnp.zeros((nz, cy), F32)
-    ys[2] = low
-    ys[3] = high
-    halo_start(1)
-    save_veloc = pltpu.make_async_copy(v_ref, veloc_out, out_sem.at[0])
-    save_veloc.start()
+    low, high = lax.fori_loop(0, nz, move_xy, (empty, empty))
+    xs[4, 0] = v_ref[1, :, 0, :]
+    xs[4, 1] = jnp.zeros((nz, cy), F32)
+    xs[5, 0] = v_ref[0, :, cx - 1, :]
+    xs[5, 1] = jnp.zeros((nz, cy), F32)
+    ys[4] = low
+    ys[5] = high
+    halo_start(2)
     halo_wait(1)
 
-    def strain(z, carry):
+    def strain_z(z, carry):
         mat = m_ref[z]
-        lame, shear, piezo = pick(mat, lame_t), pick(mat, shear_t), pick(mat, piezo_t)
+        shear, piezo = pick(mat, shear_t), pick(mat, piezo_t)
         ux, uy, uz = v_ref[0, z], v_ref[1, z], v_ref[2, z]
-        strain_x = ux - x_last(ux, 1, 0, z)
-        strain_y = uy - y_last(uy, 1, 0, z)
-        strain_z = uz - below(v_ref, 2, z)
-        spread = lame * (strain_x + strain_y + strain_z)
-        twice = 2.0 * shear
-        s_ref[0, z] = s_ref[0, z] + spread + twice * strain_x
-        s_ref[1, z] = s_ref[1, z] + spread + twice * strain_y
-        s_ref[2, z] = s_ref[2, z] + spread + twice * strain_z
-        s_ref[3, z] = s_ref[3, z] + shear * (
-            (y_next(ux, 1, 0, z) - ux) + (x_next(uy, 1, 0, z) - uy)
-        )
-        sxz = s_ref[4, z] + shear * ((above(v_ref, 0, z) - ux) + (x_next(uz, 1, 1, z) - uz))
-        syz = s_ref[5, z] + shear * ((above(v_ref, 1, z) - uy) + (y_next(uz, 1, 1, z) - uz))
+        sxz = s_ref[4, z] + shear * ((above(v_ref, 0, z) - ux) + (x_next(uz, 1, 0, z) - uz))
+        syz = s_ref[5, z] + shear * ((above(v_ref, 1, z) - uy) + (y_next(uz, 1, 0, z) - uz))
         s_ref[4, z] = sxz
         s_ref[5, z] = syz
         charge[z] = piezo * (sxz + syz)
+        return carry
+
+    def strain_xy(z, carry):
+        mat = m_ref[z]
+        lame, shear = pick(mat, lame_t), pick(mat, shear_t)
+        ux, uy, uz = v_ref[0, z], v_ref[1, z], v_ref[2, z]
+        along_x = ux - x_last(ux, 2, 0, z)
+        along_y = uy - y_last(uy, 2, 0, z)
+        along_z = uz - below(v_ref, 2, z)
+        spread = lame * (along_x + along_y + along_z)
+        twice = 2.0 * shear
+        s_ref[0, z] = s_ref[0, z] + spread + twice * along_x
+        s_ref[1, z] = s_ref[1, z] + spread + twice * along_y
+        s_ref[2, z] = s_ref[2, z] + spread + twice * along_z
+        s_ref[3, z] = s_ref[3, z] + shear * (
+            (y_next(ux, 2, 0, z) - ux) + (x_next(uy, 2, 0, z) - uy)
+        )
         return carry
 
     def raw_copy(no, which):
@@ -257,7 +273,7 @@
         )
 
     def chunk(no, carry):
-        lax.fori_loop(no * zc, no * zc + zc, strain, 0)
+        lax.fori_loop(no * zc, no * zc + zc, strain_z, 0)
         for which in range(2):
             @pl.when(gy != hubs[which])
             def _():
@@ -266,6 +282,10 @@
         return carry
 
     lax.fori_loop(0, chunks, chunk, 0)
+    save_veloc = pltpu.make_async_copy(v_ref, veloc_out, out_sem.at[0])
+    save_veloc.start()
+    halo_wait(2)
+    lax.fori_loop(0, nz, strain_xy, 0)
     save_stress = pltpu.make_async_copy(s_ref, stress_out, out_sem.at[1])
     save_stress.start()
 
@@ -388,20 +408,24 @@
 def solve_kernel(
     ny, kinds, lateral_t, normal_t,
     lines, cos_high, cos_low, sin_high, sin_low, wave_x, wave_y, stress, veloc,
-    modes, stress_out, veloc_out, high, low, sem,
+    modes, stress_out, veloc_out, high, low, s_ref, v_ref, sem,
 ):
     me = lax.axis_index("gx") * ny + lax.axis_index("gy")
     width = lines.shape[2]
     _, nz, block, _ = modes.shape
-    copies = [
-        pltpu.make_async_copy(stress, stress_out, sem.at[0]),
-        pltpu.make_async_copy(veloc, veloc_out, sem.at[1]),
+    loads = [
+        pltpu.make_async_copy(stress, s_ref, sem.at[0]),
+        pltpu.make_async_copy(veloc, v_ref, sem.at[1]),
+    ]
+    stores = [
+        pltpu.make_async_copy(s_ref, stress_out, sem.at[2]),
+        pltpu.make_async_copy(v_ref, veloc_out, sem.at[3]),
     ]
 
     @pl.when(pl.program_id(0) == 0)
     def _():
-        for copy in copies:
-            copy.start()
+        for load in loads:
+            load.start()
         for source in range(lines.shape[0]):
             value = lines[source].T
             top = value.astype(BF16)
@@ -410,6 +434,12 @@
 
     with_cos = dot3(high[...], low[...], cos_high[...], cos_low[...])
     with_sin = dot3(high[...], low[...], sin_high[...], sin_low[...])
+
+    @pl.when(pl.program_id(0) == 0)
+    def _():
+        for load, store in zip(loads, stores):
+            load.wait()
+            store.start()
 
     def part(value, z, no):
         start = (z * 2 + no) * block
@@ -442,8 +472,8 @@
 
     @pl.when(pl.program_id(0) == pl.num_programs(0) - 1)
     def _():
-        for copy in copies:
-            copy.wait()
+        for store in stores:
+            store.wait()
 
 
 def per_device(
@@ -475,10 +505,10 @@
             pltpu.VMEM(material.shape, jnp.int32),
             pltpu.VMEM(thigh.shape[1:], BF16),
             pltpu.VMEM(tlow.shape[1:], BF16),
-            pltpu.VMEM((4, 2, nz, cy), F32),
-            pltpu.VMEM((4, 2, nz, cy), F32),
-            pltpu.VMEM((4, cx, cy), F32),
-            pltpu.VMEM((4, cx, cy), F32),
+            pltpu.VMEM((6, 2, nz, cy), F32),
+            pltpu.VMEM((6, 2, nz, cy), F32),
+            pltpu.VMEM((6, cx, cy), F32),
+            pltpu.VMEM((6, cx, cy), F32),
             pltpu.VMEM((nz, cx, cy), F32),
             pltpu.VMEM((chunks, ny, zc, cx, cy), F32),
             pltpu.VMEM((zc * cx, total_y), BF16),
@@ -487,8 +517,8 @@
             pltpu.SemaphoreType.DMA((5,)),
             pltpu.SemaphoreType.DMA((2,)),
             pltpu.SemaphoreType.DMA((chunks,)),
-            pltpu.SemaphoreType.DMA((8,)),
-            pltpu.SemaphoreType.DMA((8,)),
+            pltpu.SemaphoreType.DMA((12,)),
+            pltpu.SemaphoreType.DMA((12,)),
             pltpu.SemaphoreType.DMA((chunks, 2)),
             pltpu.SemaphoreType.DMA((chunks, ny)),
             pltpu.SemaphoreType.DMA((chunks, total // 2)),
@@ -503,7 +533,7 @@
         stress, velocity, material, jnp.asarray(thigh), jnp.asarray(tlow),
     )
 
-    columns = min(256, total_x)
+    columns = min(512, total_x)
     wave_x = (2.0 * np.sin(np.pi * np.arange(total_x) / total_x)) ** 2
     wave_y = (2.0 * np.sin(np.pi * np.arange(total_y) / total_y)) ** 2
     wave_y = np.broadcast_to(wave_y.reshape(total, block, 1), (total, block, 128))
@@ -529,7 +559,9 @@
         scratch_shapes=[
             pltpu.VMEM((chunks * width, total_x), BF16),
             pltpu.VMEM((chunks * width, total_x), BF16),
-            pltpu.SemaphoreType.DMA((2,)),
+            pltpu.VMEM(stress.shape, F32),
+            pltpu.VMEM(velocity.shape, F32),
+            pltpu.SemaphoreType.DMA((4,)),
         ],
         compiler_params=pltpu.CompilerParams(vmem_limit_bytes=56 * 2**20),
         name="lines_and_solve",

time: 199 us -> 58.9 us (0.30)
  Pallas kernels: 198 us -> 58.1 us
    pallas_call x1, Pallas kernels: 147 us -> 7.01 us  [per_device(): pl.pallas_call(functools.partial(solve_kernel, ny), grid=(total_x // colu...]
where the time goes in v3:
time: 58.9 us; the launch traced here: 58.7 us
  Pallas kernels  58.1 us (99%)
  between operations  0.64 us (1%)
    pallas_call x1, Pallas kernels, per_device(): pl.pallas_call(functools.partial(step_kernel, nx, ny), out_shape=(jax.Sha...  51.1 us
    pallas_call x1, Pallas kernels, per_device(): pl.pallas_call(functools.partial(solve_kernel, ny), grid=(total_x // colu...  7.01 us

profile of v3, /device:TPU:0, one launch (start us, length us, event | category | flops | bytes accessed | tf_op | source)
XLA Modules:
  0.0 58.7 jit_solution(10799278136258249470)
XLA Ops:
  0.6 51.1 %elastic_and_lines.1 = (f32[6,16,64,128]{3,2,1,0:T(8,128)}, f32[3,16,64,128]{3,2,1,0:T(8,128)}, f32[4,512,128]{2,1,0:T(8,128)}) custom-call(f32[3]{0:T(128)} %buoy_t.1, f32[3]{0:T(128)} %lame_t.1, f32[3]{0:T(128)} %shear_t.1, f32[3]{0:T(128)} %piezo_t.1, f32[6,16,64,128]{3,2,1,0:T(8,128)} %stress_in.1, f32[3,16,64,128]{3,2,1,0:T(8,128)} %veloc_in.1, ...), custom_call_target="tpu_custom_call" | custom-call | tf_op jit(solution)/shard_map/elastic_and_lines/pallas_call | solution.py:493
  51.7 7.0 %lines_and_solve.1 = (f32[2,16,16,512]{3,2,1,0:T(8,128)}, f32[6,16,64,128]{3,2,1,0:T(8,128)}, f32[3,16,64,128]{3,2,1,0:T(8,128)}) custom-call(s32[16]{0:T(128)} %kinds.1, f32[3]{0:T(128)} %lateral_t.1, f32[3]{0:T(128)} %normal_t.1, f32[4,512,128]{2,1,0:T(8,128)} %get-tuple-element.9.lines, bf16[512,512]{1,0:T(8,128)(2,1)} %constant.18.clone.cos_high, ...), custom_call_target="tpu_custom_call" | custom-call | tf_op jit(solution)/shard_map/lines_and_solve/pallas_call | solution.py:541

commit v4 on v3

--- a/solution.py
+++ b/solution.py
@@ -34,10 +34,11 @@
 
 @functools.lru_cache(maxsize=2)
 def tables_x(total_x):
+    half = total_x // 2
     place = np.arange(total_x)
-    angle = 2.0 * np.pi / total_x * (place[:, None] * place[None, :] % total_x)
-    scale = 1.0 / math.sqrt(total_x)
-    return split_table(np.cos(angle) * scale) + split_table(np.sin(angle) * scale)
+    angle = 2.0 * np.pi / total_x * (place[:, None] * place[None, :half] % total_x)
+    both = np.stack([np.cos(angle), np.sin(angle)]) / math.sqrt(total_x)
+    return split_table(both.reshape(2, half, 2, half).transpose(2, 0, 1, 3))
 
 
 def pick(codes, table):
@@ -272,12 +273,28 @@
             device_id_type=MESH,
         )
 
-    def chunk(no, carry):
-        lax.fori_loop(no * zc, no * zc + zc, strain_z, 0)
+    def raw_start(no):
         for which in range(2):
             @pl.when(gy != hubs[which])
             def _():
                 raw_copy(no, which).start()
+
+    def raw_next(no):
+        for which in range(2):
+            @pl.when(gy != hubs[which])
+            def _():
+                raw_copy(no, which).wait_send()
+
+        @pl.when(no + 1 < chunks)
+        def _():
+            raw_start(no + 1)
+
+    def chunk(no, carry):
+        lax.fori_loop(no * zc, no * zc + zc, strain_z, 0)
+
+        @pl.when(no == 0)
+        def _():
+            raw_start(no)
 
         return carry
 
@@ -333,6 +350,7 @@
     @pl.when(is_hub)
     def _():
         def hub_chunk(no, carry):
+            raw_next(no)
             store_cols(gy, charge[pl.ds(no * zc, zc)])
 
             def take(step, carry):
@@ -385,12 +403,15 @@
 
         lax.fori_loop(0, chunks, finish_sends, 0)
 
+    @pl.when(jnp.logical_not(is_hub))
+    def _():
+        def step(no, carry):
+            raw_next(no)
+            return carry
+
+        lax.fori_loop(0, chunks, step, 0)
+
     def finish(no, carry):
-        for which in range(2):
-            @pl.when(gy != hubs[which])
-            def _():
-                raw_copy(no, which).wait_send()
-
         def finish_source(source, carry):
             @pl.when(jnp.logical_not(jnp.logical_and(source == gx, is_hub)))
             def _():
@@ -406,40 +427,49 @@
 
 
 def solve_kernel(
-    ny, kinds, lateral_t, normal_t,
-    lines, cos_high, cos_low, sin_high, sin_low, wave_x, wave_y, stress, veloc,
-    modes, stress_out, veloc_out, high, low, s_ref, v_ref, sem,
+    ny, kinds, lateral_t, normal_t, wave_x, wave_y,
+    lines_in, thigh_in, tlow_in, stress, veloc,
+    modes, stress_out, veloc_out,
+    lines, thigh, tlow, high, low, s_ref, v_ref, sem,
 ):
     me = lax.axis_index("gx") * ny + lax.axis_index("gy")
-    width = lines.shape[2]
+    chunks, total_x, width = lines.shape
     _, nz, block, _ = modes.shape
     loads = [
-        pltpu.make_async_copy(stress, s_ref, sem.at[0]),
-        pltpu.make_async_copy(veloc, v_ref, sem.at[1]),
+        pltpu.make_async_copy(src, dst, sem.at[no])
+        for no, (src, dst) in enumerate(
+            [(lines_in, lines), (thigh_in, thigh), (tlow_in, tlow), (stress, s_ref), (veloc, v_ref)]
+        )
     ]
     stores = [
-        pltpu.make_async_copy(s_ref, stress_out, sem.at[2]),
-        pltpu.make_async_copy(v_ref, veloc_out, sem.at[3]),
+        pltpu.make_async_copy(s_ref, stress_out, sem.at[5]),
+        pltpu.make_async_copy(v_ref, veloc_out, sem.at[6]),
     ]
-
-    @pl.when(pl.program_id(0) == 0)
-    def _():
-        for load in loads:
-            load.start()
-        for source in range(lines.shape[0]):
-            value = lines[source].T
+    for load in loads:
+        load.start()
+    loads[0].wait()
+    for source in range(chunks):
+        for parity in range(2):
+            value = lines[source, pl.ds(parity, total_x // 2, stride=2), :].T
             top = value.astype(BF16)
-            high[source * width : (source + 1) * width, :] = top
-            low[source * width : (source + 1) * width, :] = (value - top.astype(F32)).astype(BF16)
-
-    with_cos = dot3(high[...], low[...], cos_high[...], cos_low[...])
-    with_sin = dot3(high[...], low[...], sin_high[...], sin_low[...])
-
-    @pl.when(pl.program_id(0) == 0)
-    def _():
-        for load, store in zip(loads, stores):
-            load.wait()
-            store.start()
+            high[parity, source * width : (source + 1) * width, :] = top
+            low[parity, source * width : (source + 1) * width, :] = (
+                value - top.astype(F32)
+            ).astype(BF16)
+    loads[1].wait()
+    loads[2].wait()
+
+    def product(kind):
+        even, odd = (
+            dot3(high[parity], low[parity], thigh[parity, kind], tlow[parity, kind])
+            for parity in range(2)
+        )
+        return jnp.concatenate([even + odd, even - odd], axis=1)
+
+    with_cos, with_sin = product(0), product(1)
+    for load, store in zip(loads[3:], stores):
+        load.wait()
+        store.start()
 
     def part(value, z, no):
         start = (z * 2 + no) * block
@@ -470,10 +500,8 @@
         modes[0, z] = real
         modes[1, z] = imag
 
-    @pl.when(pl.program_id(0) == pl.num_programs(0) - 1)
-    def _():
-        for store in stores:
-            store.wait()
+    for store in stores:
+        store.wait()
 
 
 def per_device(
@@ -533,43 +561,37 @@
         stress, velocity, material, jnp.asarray(thigh), jnp.asarray(tlow),
     )
 
-    columns = min(512, total_x)
     wave_x = (2.0 * np.sin(np.pi * np.arange(total_x) / total_x)) ** 2
     wave_y = (2.0 * np.sin(np.pi * np.arange(total_y) / total_y)) ** 2
     wave_y = np.broadcast_to(wave_y.reshape(total, block, 1), (total, block, 128))
-    table_spec = pl.BlockSpec((total_x, columns), lambda i: (0, i))
+    vmem = pl.BlockSpec(memory_space=pltpu.VMEM)
+    half = total_x // 2
+    xhigh, xlow = tables_x(total_x)
     modes, stress_next, velocity_next = pl.pallas_call(
         functools.partial(solve_kernel, ny),
-        grid=(total_x // columns,),
         out_shape=(
             jax.ShapeDtypeStruct((2, nz, block, total_x), F32),
             jax.ShapeDtypeStruct(stress.shape, F32),
             jax.ShapeDtypeStruct(velocity.shape, F32),
         ),
-        in_specs=[smem] * 3
-        + [pl.BlockSpec((chunks, total_x, width), lambda i: (0, 0, 0))]
-        + [table_spec] * 4
-        + [
-            pl.BlockSpec((1, columns), lambda i: (0, i)),
-            pl.BlockSpec((total, block, 128), lambda i: (0, 0, 0)),
-            hbm,
-            hbm,
-        ],
-        out_specs=(pl.BlockSpec((2, nz, block, columns), lambda i: (0, 0, 0, i)), hbm, hbm),
+        in_specs=[smem] * 3 + [vmem] * 2 + [hbm] * 5,
+        out_specs=(vmem, hbm, hbm),
         scratch_shapes=[
-            pltpu.VMEM((chunks * width, total_x), BF16),
-            pltpu.VMEM((chunks * width, total_x), BF16),
+            pltpu.VMEM((chunks, total_x, width), F32),
+            pltpu.VMEM(xhigh.shape, BF16),
+            pltpu.VMEM(xlow.shape, BF16),
+            pltpu.VMEM((2, chunks * width, half), BF16),
+            pltpu.VMEM((2, chunks * width, half), BF16),
             pltpu.VMEM(stress.shape, F32),
             pltpu.VMEM(velocity.shape, F32),
-            pltpu.SemaphoreType.DMA((4,)),
+            pltpu.SemaphoreType.DMA((7,)),
         ],
         compiler_params=pltpu.CompilerParams(vmem_limit_bytes=56 * 2**20),
         name="lines_and_solve",
     )(
-        layer_kind, permit_lateral, permit_normal, lines,
-        *[jnp.asarray(table) for table in tables_x(total_x)],
+        layer_kind, permit_lateral, permit_normal,
         jnp.asarray(wave_x.reshape(1, -1), F32), jnp.asarray(wave_y, F32),
-        stress_next, velocity_next,
+        lines, jnp.asarray(xhigh), jnp.asarray(xlow), stress_next, velocity_next,
     )
     return stress_next, velocity_next, modes
 

time: 58.9 us -> 58.1 us (0.986)
  Pallas kernels: 58.1 us -> 57.3 us
where the time goes in v4:
time: 58.1 us; the launch traced here: 58 us
  Pallas kernels  57.3 us (99%)
  between operations  0.64 us (1%)
    pallas_call x1, Pallas kernels, per_device(): pl.pallas_call(functools.partial(step_kernel, nx, ny), out_shape=(jax.Sha...  50.6 us
    pallas_call x1, Pallas kernels, per_device(): pl.pallas_call(functools.partial(solve_kernel, ny), out_shape=(jax.ShapeD...  6.74 us

profile of v4, /device:TPU:0, one launch (start us, length us, event | category | flops | bytes accessed | tf_op | source)
XLA Modules:
  0.0 58.0 jit_solution(5475467890211435416)
XLA Ops:
  0.6 50.6 %elastic_and_lines.1 = (f32[6,16,64,128]{3,2,1,0:T(8,128)}, f32[3,16,64,128]{3,2,1,0:T(8,128)}, f32[4,512,128]{2,1,0:T(8,128)}) custom-call(f32[3]{0:T(128)} %buoy_t.1, f32[3]{0:T(128)} %lame_t.1, f32[3]{0:T(128)} %shear_t.1, f32[3]{0:T(128)} %piezo_t.1, f32[6,16,64,128]{3,2,1,0:T(8,128)} %stress_in.1, f32[3,16,64,128]{3,2,1,0:T(8,128)} %veloc_in.1, ...), custom_call_target="tpu_custom_call" | custom-call | tf_op jit(solution)/shard_map/elastic_and_lines/pallas_call | solution.py:521
  51.2 6.7 %lines_and_solve.1 = (f32[2,16,16,512]{3,2,1,0:T(8,128)}, f32[6,16,64,128]{3,2,1,0:T(8,128)}, f32[3,16,64,128]{3,2,1,0:T(8,128)}) custom-call(s32[16]{0:T(128)} %kinds.1, f32[3]{0:T(128)} %lateral_t.1, f32[3]{0:T(128)} %normal_t.1, f32[1,512]{1,0:T(1,128)} %constant.14.clone.wave_x, f32[32,16,128]{2,1,0:T(8,128)} %constant.15.clone.wave_y, ...), custom_call_target="tpu_custom_call" | custom-call | tf_op jit(solution)/shard_map/lines_and_solve/pallas_call | solution.py:570

commit v5 on v4

--- a/solution.py
+++ b/solution.py
@@ -429,8 +429,8 @@
 def solve_kernel(
     ny, kinds, lateral_t, normal_t, wave_x, wave_y,
     lines_in, thigh_in, tlow_in, stress, veloc,
-    modes, stress_out, veloc_out,
-    lines, thigh, tlow, high, low, s_ref, v_ref, sem,
+    modes_out, stress_out, veloc_out,
+    modes, lines, thigh, tlow, high, low, s_ref, v_ref, sem, modes_sem,
 ):
     me = lax.axis_index("gx") * ny + lax.axis_index("gy")
     chunks, total_x, width = lines.shape
@@ -466,10 +466,11 @@
         )
         return jnp.concatenate([even + odd, even - odd], axis=1)
 
-    with_cos, with_sin = product(0), product(1)
+    with_cos = product(0)
     for load, store in zip(loads[3:], stores):
         load.wait()
         store.start()
+    with_sin = product(1)
 
     def part(value, z, no):
         start = (z * 2 + no) * block
@@ -499,6 +500,9 @@
             imag = imags[z] + factors[z] * imag
         modes[0, z] = real
         modes[1, z] = imag
+        store = pltpu.make_async_copy(modes.at[:, z], modes_out.at[:, z], modes_sem.at[z])
+        store.start()
+        stores.append(store)
 
     for store in stores:
         store.wait()
@@ -575,8 +579,9 @@
             jax.ShapeDtypeStruct(velocity.shape, F32),
         ),
         in_specs=[smem] * 3 + [vmem] * 2 + [hbm] * 5,
-        out_specs=(vmem, hbm, hbm),
+        out_specs=(hbm, hbm, hbm),
         scratch_shapes=[
+            pltpu.VMEM((2, nz, block, total_x), F32),
             pltpu.VMEM((chunks, total_x, width), F32),
             pltpu.VMEM(xhigh.shape, BF16),
             pltpu.VMEM(xlow.shape, BF16),
@@ -585,6 +590,7 @@
             pltpu.VMEM(stress.shape, F32),
             pltpu.VMEM(velocity.shape, F32),
             pltpu.SemaphoreType.DMA((7,)),
+            pltpu.SemaphoreType.DMA((nz,)),
         ],
         compiler_params=pltpu.CompilerParams(vmem_limit_bytes=56 * 2**20),
         name="lines_and_solve",

time: 58.1 us -> 57.6 us (level)
  no operation moved by 1% of the time
where the time goes in v5:
time: 57.6 us; the launch traced here: 57.4 us
  Pallas kernels  56.8 us (99%)
  between operations  0.64 us (1%)
    pallas_call x1, Pallas kernels, per_device(): pl.pallas_call(functools.partial(step_kernel, nx, ny), out_shape=(jax.Sha...  50.6 us
    pallas_call x1, Pallas kernels, per_device(): pl.pallas_call(functools.partial(solve_kernel, ny), out_shape=(jax.ShapeD...  6.19 us

profile of v5, /device:TPU:0, one launch (start us, length us, event | category | flops | bytes accessed | tf_op | source)
XLA Modules:
  0.0 57.4 jit_solution(1875535701033961832)
XLA Ops:
  0.6 50.6 %elastic_and_lines.1 = (f32[6,16,64,128]{3,2,1,0:T(8,128)}, f32[3,16,64,128]{3,2,1,0:T(8,128)}, f32[4,512,128]{2,1,0:T(8,128)}) custom-call(f32[3]{0:T(128)} %buoy_t.1, f32[3]{0:T(128)} %lame_t.1, f32[3]{0:T(128)} %shear_t.1, f32[3]{0:T(128)} %piezo_t.1, f32[6,16,64,128]{3,2,1,0:T(8,128)} %stress_in.1, f32[3,16,64,128]{3,2,1,0:T(8,128)} %veloc_in.1, ...), custom_call_target="tpu_custom_call" | custom-call | tf_op jit(solution)/shard_map/elastic_and_lines/pallas_call | solution.py:525
  51.2 6.2 %lines_and_solve.1 = (f32[2,16,16,512]{3,2,1,0:T(8,128)}, f32[6,16,64,128]{3,2,1,0:T(8,128)}, f32[3,16,64,128]{3,2,1,0:T(8,128)}) custom-call(s32[16]{0:T(128)} %kinds.1, f32[3]{0:T(128)} %lateral_t.1, f32[3]{0:T(128)} %normal_t.1, f32[1,512]{1,0:T(1,128)} %constant.14.clone.wave_x, f32[32,16,128]{2,1,0:T(8,128)} %constant.15.clone.wave_y, ...), custom_call_target="tpu_custom_call" | custom-call | tf_op jit(solution)/shard_map/lines_and_solve/pallas_call | solution.py:574
